TPU v7x, 128 devices: a whole 4x4x4 slice. The times are simulated.
128 devices in a mesh: mp: 4 (over z_hi, core), dp: 32 (over y, x, z_lo).
Axes of the slice: x: 4, y: 4, z: 4 (z_hi: 2, z_lo: 2; z = z_hi * 2 + z_lo), core: 2. Of those that a mesh axis runs over, the one named last changes fastest.
Arguments:
- tokens: bfloat16 [512, 64, 1024], P('dp'), may hold values from -10 to 10
- norm_gain: float32 [1024], replicated, may hold values from 0.1 to 1.9
- weight_in: bfloat16 [1024, 4096], P(None, 'mp'), may hold values from -0.1875 to 0.1875
- weight_out: bfloat16 [4096, 1024], P('mp'), may hold values from -0.09375 to 0.09375
- final_gain: float32 [1024], replicated, may hold values from 0.1 to 1.9
- centres: bfloat16 [1048576, 1024], P(('mp', 'dp')), may hold values from -7 to 7
- labels: int32 [512], P('dp'), may hold values from 0 to 1048575
Outputs:
- row_loss: float32 [512], P('dp')
- feat_grad: float32 [512, 1024], P('dp', 'mp')
All inputs are finite; a program needn't handle non-finite values.
Results may differ from a plain program's by a relative error of at most 0.0038.
Values may be sent and summed in bfloat16 or wider, within the bound.
No kernel may reach another device: no remote copies, remote signals or barrier semaphores. Data moves between devices by JAX's collectives and lax.ppermute only.
A program may use at most 128 MiB of HBM per device.

v0:
```python
import math

import jax
import jax.numpy as jnp
from jax import lax
from jax.sharding import PartitionSpec as P

logit_scale = 64.0
angle_margin = 0.5


def layer_norm(values, gain_vec):
    average = jnp.mean(values, axis=-1, keepdims=True)
    centred = values - average
    variance = jnp.mean(centred * centred, axis=-1, keepdims=True)
    return centred * lax.rsqrt(variance + 1e-06) * gain_vec


def arc_target(target_cos):
    target_sine = jnp.sqrt(jnp.maximum(1.0 - target_cos * target_cos, 0.01))
    inside = target_cos > -math.cos(angle_margin)
    shifted = jnp.where(
        inside,
        target_cos * math.cos(angle_margin) - target_sine * math.sin(angle_margin),
        target_cos - angle_margin * math.sin(angle_margin),
    )
    margin_slope = jnp.where(
        inside, math.cos(angle_margin) + math.sin(angle_margin) * target_cos / target_sine, 1.0
    )
    return (shifted, margin_slope)


def shards(tokens, norm_gain, weight_in, weight_out, final_gain, centres, labels):
    images, tok_count, model_width = tokens.shape
    tokens_wide = tokens.astype(jnp.float32)
    normed = layer_norm(tokens_wide, norm_gain).astype(jnp.bfloat16).reshape(-1, model_width)
    hidden = jax.nn.gelu(
        jnp.dot(normed, weight_in, preferred_element_type=jnp.float32), approximate=False
    ).astype(jnp.bfloat16)
    branch = jnp.dot(hidden, weight_out, preferred_element_type=jnp.float32).reshape(
        images, tok_count, model_width
    )
    partial_value = jnp.mean(branch, axis=1)
    pooled = jnp.mean(tokens_wide, axis=1) + lax.psum(partial_value, "mp")
    embedding = layer_norm(pooled, final_gain)
    length = jnp.sqrt(jnp.sum(embedding * embedding, axis=1) + 1e-06)
    unit_rows = (embedding / length[:, None]).astype(jnp.bfloat16)
    centre_wide = centres.astype(jnp.float32)
    centre_unit = (
        centre_wide * lax.rsqrt(jnp.sum(centre_wide * centre_wide, axis=1, keepdims=True) + 1e-06)
    ).astype(jnp.bfloat16)
    cls_count = centres.shape[0]
    offset = (lax.axis_index("mp") * lax.axis_size("dp") + lax.axis_index("dp")) * cls_count
    gathered = lax.all_gather(unit_rows, "dp", axis=0, tiled=True)
    all_labels = lax.all_gather(labels, "dp", axis=0, tiled=True)
    cosine = lax.dot_general(
        gathered, centre_unit, (((1,), (1,)), ((), ())), preferred_element_type=jnp.float32
    )
    local_label = all_labels - offset
    picked = local_label[:, None] == lax.broadcasted_iota(jnp.int32, cosine.shape, 1)
    target_cos = jnp.sum(jnp.where(picked, cosine, 0.0), axis=1)
    shifted, margin_slope = arc_target(target_cos)
    logits = jnp.where(picked, logit_scale * shifted[:, None], logit_scale * cosine)
    is_owner = jnp.any(picked, axis=1)
    exponent = jnp.exp(logits)
    totals, target = lax.psum(
        (jnp.sum(exponent, axis=1), jnp.where(is_owner, logit_scale * shifted, 0.0)), ("mp", "dp")
    )
    losses_all = jnp.log(totals) - target
    row_loss = lax.dynamic_slice_in_dim(losses_all, lax.axis_index("dp") * images, images, 0)
    probability = exponent / totals[:, None]
    weights = (
        logit_scale * jnp.where(picked, (probability - 1.0) * margin_slope[:, None], probability)
    ).astype(jnp.bfloat16)
    grad_term = jnp.dot(weights, centre_unit, preferred_element_type=jnp.float32)
    own_grad = lax.psum_scatter(grad_term, "dp", scatter_dimension=0, tiled=True)
    own_grad = lax.psum_scatter(own_grad, "mp", scatter_dimension=1, tiled=True)
    col_count = model_width // lax.axis_size("mp")
    unit_own = lax.dynamic_slice_in_dim(
        unit_rows.astype(jnp.float32), lax.axis_index("mp") * col_count, col_count, 1
    )
    inner_dots = lax.psum(jnp.sum(unit_own * own_grad, axis=1), "mp")
    own_grad = own_grad - unit_own * inner_dots[:, None]
    feat_grad = own_grad / length[:, None]
    return (row_loss, feat_grad)


def solution(mesh):
    return jax.shard_map(
        shards,
        mesh=mesh,
        in_specs=(
            P("dp", None, None),
            P(),
            P(None, "mp"),
            P("mp", None),
            P(),
            P(("mp", "dp"), None),
            P("dp"),
        ),
        out_specs=(P("dp"), P("dp", "mp")),
        check_vma=False,
    )
```

profile of v0, /device:TPU:0, one launch (start us, length us, event | category | flops | bytes accessed | tf_op | source)
XLA Modules:
  0.0 539.6 jit_solution(13666363619208670317)
XLA Ops:
  7.2 2.3 convert_reduce_fusion.1
  9.6 2.3 fusion.10
  11.9 2.0 fusion.12
  14.0 14.5 %bitcast_reduce_fusion = f32[16,1024]{1,0:T(8,128)S(1)} fusion(bf16[1024,1024]{1,0:T(8,128)(2,1)S(1)} %copy-done, bf16[1024,1024]{1,0:T(8,128)(2,1)} %bitcast.8, bf16[1024,1024]{1,0:T(8,128)(2,1)} %param.9), kind=kOutput, calls=%fused_computation.24 | convolution fusion | flops 4364156928 | bytes 6356992 | tf_op jit(solution)/shard_map/dot_general | solution.py:40
  28.5 0.6 broadcast_multiply_fusion
  29.2 42.4 %all-reduce.4.cloned.1.call-done = f32[16,1024]{1,0:T(8,128)} async-done(((f32[16,1024]{1,0:T(8,128)}), f32[16,1024]{1,0:T(8,128)}) %all-reduce.4.cloned.1.call-update) | async-done | bytes 65552 | tf_op jit(solution)/shard_map/psum | solution.py:44
  71.6 1.0 fusion.62
  73.0 0.7 divide_convert_fusion
  73.8 0.6 dynamic-slice
  75.0 0.2 dynamic-update-slice
  75.3 19.0 %all-reduce = s32[512]{0:T(512)S(1)} all-reduce(s32[512]{0:T(512)S(1)} %dynamic-update-slice), channel_id=1, replica_groups=mesh['mp'=4,'dp'=32] {'dp'}, use_global_device_ids=true, to_apply=%add | all-reduce | flops 512 | bytes 4096
  94.3 7.2 %fusion = f32[8192]{0:T(1024)S(1)} fusion(bf16[8192,1024]{1,0:T(8,128)(2,1)} %param.12), kind=kLoop, calls=%fused_computation.2 | loop fusion | flops 25157632 | bytes 16809984 | tf_op jit(solution)/shard_map/reduce_sum | solution.py:50
  101.5 2.5 fusion.2
  104.0 119.8 %all-gather.2.cloned.1.call-done = bf16[512,1024]{1,0:T(8,128)(2,1)} async-done(((bf16[16,1024]{1,0:T(8,128)(2,1)}), bf16[512,1024]{1,0:T(8,128)(2,1)}) %all-gather.2.cloned.1.call-update) | async-done | bytes 1048592 | tf_op jit(solution)/shard_map/all_gather | solution.py:54
  223.8 16.7 %select_reduce_fusion = (f32[512]{0:T(512)S(1)}, f32[512,8192]{1,0:T(8,128)}) fusion(s32[512]{0:T(512)S(1)} %broadcast_subtract_fusion, bf16[512,1024]{1,0:T(8,128)(2,1)} %all-gather.2.cloned.1.call-done, bf16[8192,1024]{1,0:T(8,128)(2,1)} %param.12, f32[8192]{0:T(1024)S(1)} %add_rsqrt_fusion), kind=kOutput, calls=%fused_computation.6 | convolution fusion | flops 8627683328 | bytes 34639872 | tf_op jit(solution)/shard_map/dot_general | solution.py:56
  240.4 8.1 %fusion.3 = f32[512]{0:T(512)S(1)} fusion(f32[512,8192]{1,0:T(8,128)} %get-tuple-element.12, f32[512]{0:T(512)S(1)} %get-tuple-element.7, s32[512]{0:T(512)S(1)} %broadcast_subtract_fusion), kind=kLoop, calls=%fused_computation.9 | loop fusion | flops 16776704 | bytes 16783360 | tf_op jit(solution)/shard_map/reduce_sum | solution.py:67
  248.5 64.5 %all-reduce.1 = (f32[512]{0:T(512)S(1)}, f32[512]{0:T(512)S(1)}) all-reduce(f32[512]{0:T(512)S(1)} %get-tuple-element.6, f32[512]{0:T(512)S(1)} %fusion.3), channel_id=1, replica_groups=mesh['mp'=4,'dp'=32] {'mp','dp'}, use_global_device_ids=true, to_apply=%region_13.14 | all-reduce | flops 1024 | bytes 8192 | tf_op jit(solution)/shard_map/psum | solution.py:66
  313.1 24.6 %fusion.4 = f32[512,1024]{1,0:T(8,128)} fusion(f32[512,8192]{1,0:T(8,128)} %get-tuple-element.12, f32[512]{0:T(512)S(1)} %get-tuple-element.10, f32[512]{0:T(512)S(1)} %get-tuple-element.5, f32[512]{0:T(512)S(1)} %get-tuple-element.7, s32[512]{0:T(512)S(1)} %broadcast_subtract_fusion, bf16[8192,1024]{1,0:T(8,128)(2,1)} %param.12, f32[8192]{0:T(1024)S(1)} %add_rsqrt_fusion), kind=kOutput, calls=%fused_computation.10 | convolution fusion | flops 8652849152 | bytes 35692544 | tf_op jit(solution)/shard_map/dot_general | solution.py:75
  337.8 160.9 %reduce-scatter.3.cloned.1.call-done = f32[16,1024]{1,0:T(8,128)} async-done(((f32[512,1024]{1,0:T(8,128)}), f32[16,1024]{1,0:T(8,128)}) %reduce-scatter.3.cloned.1.call-update) | async-done | bytes 65552 | tf_op jit(solution)/shard_map/reduce_scatter | solution.py:76
  498.7 0.6 dynamic_slice.6
  499.3 24.2 %reduce-scatter.5.cloned.1.call-done = f32[16,256]{1,0:T(8,128)} async-done(((f32[16,1024]{1,0:T(8,128)}), f32[16,256]{1,0:T(8,128)}) %reduce-scatter.5.cloned.1.call-update) | async-done | bytes 16400 | tf_op jit(solution)/shard_map/reduce_scatter | solution.py:77
  523.6 0.8 fusion.29
  524.4 7.3 %psum.31 = f32[16]{0:T(128)S(1)} all-reduce(f32[16]{0:T(128)S(1)} %fusion.29), channel_id=1, replica_groups=mesh['mp'=4,'dp'=32] {'mp'}, use_global_device_ids=true, to_apply=%region_17.18 | all-reduce | flops 16 | bytes 128 | tf_op jit(solution)/shard_map/psum | solution.py:82
  531.6 1.4 fusion.28
  (34 shorter events, 0.7 us)
Async XLA Ops:
  7.2 6.8 %copy-start = (bf16[1024,1024]{1,0:T(8,128)(2,1)S(1)}, bf16[1024,1024]{1,0:T(8,128)(2,1)}, u32[]{:S(2)}) copy-start(bf16[1024,1024]{1,0:T(8,128)(2,1)} %param.10) | copy-start | bytes 6291460
  7.2 4.7 copy-start.4
  7.2 64.4 %all-reduce.4.cloned.1.call-start = ((), (), s32[]{:S(2)}) async-start(), calls=%async_computation.2 | async-start | bytes 131072 | tf_op jit(solution)/shard_map/psum | solution.py:44
  7.2 4.7 copy-start.1
  13.9 58.8 %copy-start.3 = (f32[1024]{0:T(1024)S(1)}, f32[1024]{0:T(1024)}, u32[]{:S(2)}) copy-start(f32[1024]{0:T(1024)} %param.11) | copy-start | bytes 12292
  13.9 59.8 %copy-start.6 = (u32[128]{0:T(128)S(1)}, u32[128]{0:T(128)}, u32[]{:S(2)}) copy-start(u32[128]{0:T(128)} %constant.126) | copy-start | bytes 1540
  13.9 61.1 %copy-start.5 = (s32[16]{0:T(128)S(1)}, s32[16]{0:T(128)}, u32[]{:S(2)}) copy-start(s32[16]{0:T(128)} %param.13) | copy-start | bytes 196
  29.1 194.6 %all-gather.2.cloned.1.call-start = ((), (), s32[]{:S(2)}) async-start(), calls=%async_computation.3 | async-start | bytes 1081344 | tf_op jit(solution)/shard_map/all_gather | solution.py:54
  73.7 425.0 %reduce-scatter.3.cloned.1.call-start = ((), (), s32[]{:S(2)}) async-start(), calls=%async_computation.4 | async-start | bytes 2162688 | tf_op jit(solution)/shard_map/reduce_scatter | solution.py:76
  313.1 210.5 %copy-start.2 = (bf16[16,1024]{1,0:T(8,128)(2,1)S(1)}, bf16[16,1024]{1,0:T(8,128)(2,1)}, u32[]{:S(2)}) copy-start(bf16[16,1024]{1,0:T(8,128)(2,1)} %divide_convert_fusion) | copy-start | bytes 98308
  337.7 185.9 %reduce-scatter.5.cloned.1.call-start = ((), (), s32[]{:S(2)}) async-start(), calls=%async_computation.5 | async-start | bytes 81920 | tf_op jit(solution)/shard_map/reduce_scatter | solution.py:77
Sparse Core Ops, SparseCore 0:
  29.2 42.3 all-reduce.3
  73.8 149.9 all-gather.1
  337.8 160.8 reduce-scatter.2
  501.1 22.4 reduce-scatter.4
where the time goes:
time: 541 us; the launch traced here: 540 us
  waiting for transfers between devices  347 us (64%)
  blocking collectives  90.8 us (17%)
  matrix products  55.8 us (10%)
  other arithmetic  29.4 us (5%)
  between operations  14.6 us (3%)
    reduce_scatter x1, waiting for transfers between devices, shards(): lax.psum_scatter(grad_term, 'dp', scatter_dimension=0, tiled=True)  161 us
    all_gather x1, waiting for transfers between devices, shards(): gathered = lax.all_gather(unit_rows, 'dp', axis=0, tiled=True)  120 us
    psum x1, blocking collectives, shards(): lax.psum((jnp.sum(exponent, axis=1), jnp.where(is_owner, logit_scale * sh...  64.5 us
    psum x1, waiting for transfers between devices, shards(): pooled = jnp.mean(tokens_wide, axis=1) + lax.psum(partial_value, 'mp')  42.4 us
    dot_general x1, matrix products, shards(): jnp.dot(weights, centre_unit, preferred_element_type=jnp.float32)  24.6 us
    reduce_scatter x1, waiting for transfers between devices, shards(): own_grad = lax.psum_scatter(own_grad, 'mp', scatter_dimension=1, tiled=True)  24.2 us
    unnamed x1, blocking collectives  19 us
    dot_general x1, matrix products, shards(): lax.dot_general(gathered, centre_unit, (((1,), (1,)), ((), ())), preferre...  16.7 us
  transfers between devices with their start and end apart: 4, of which 4 were waited for; matrix products, arithmetic and copies ran while one was open for 2% of the time, Pallas kernels for 0%

commit v1 on v0

v1 whole, which is shorter than its diff:
```python
import math

import jax
import jax.numpy as jnp
from jax import lax
from jax.experimental import pallas as pl
from jax.experimental.pallas import tpu as pltpu
from jax.sharding import Mesh, PartitionSpec as P

logit_scale = 64.0
angle_margin = 0.5
exp2_scale = logit_scale / math.log(2.0)
vmem_limit = 56 * 1024 * 1024
lanes = 128
f32 = jnp.float32
bf16 = jnp.bfloat16


def params(**kw):
    return pltpu.CompilerParams(vmem_limit_bytes=vmem_limit, **kw)


def arc_target(target_cos):
    target_sine = jnp.sqrt(jnp.maximum(1.0 - target_cos * target_cos, 0.01))
    inside = target_cos > -math.cos(angle_margin)
    shifted = jnp.where(
        inside,
        target_cos * math.cos(angle_margin) - target_sine * math.sin(angle_margin),
        target_cos - angle_margin * math.sin(angle_margin),
    )
    margin_slope = jnp.where(
        inside, math.cos(angle_margin) + math.sin(angle_margin) * target_cos / target_sine, 1.0
    )
    return (shifted, margin_slope)


def layer_norm(values, gain_vec):
    average = jnp.mean(values, axis=-1, keepdims=True)
    centred = values - average
    variance = jnp.mean(centred * centred, axis=-1, keepdims=True)
    return centred * lax.rsqrt(variance + 1e-06) * gain_vec


def split3(value):
    hi = value.astype(bf16).astype(f32)
    mid = (value - hi).astype(bf16).astype(f32)
    return hi, mid, value - hi - mid


def ffn_kernel(tokens_ref, gain_ref, win_ref, wout_ref, out_ref, mean_ref, tok_ref):
    step = pl.program_id(0)
    block, width = tokens_ref.shape
    toks = 64
    per = block // toks
    wide = tokens_ref[...].astype(f32)
    normed = layer_norm(wide, gain_ref[...]).astype(bf16)
    pre = jnp.dot(normed, win_ref[...], preferred_element_type=f32)
    hidden = (0.5 * pre * (1.0 + lax.erf(pre * math.sqrt(0.5)))).astype(bf16).astype(f32)
    for k in range(per):
        mean_ref[pl.ds(step * per + k, 1), :] = (
            jnp.sum(hidden[k * toks : (k + 1) * toks], axis=0, keepdims=True) * (1.0 / toks)
        )
        tok_ref[pl.ds(step * per + k, 1), :] = (
            jnp.sum(wide[k * toks : (k + 1) * toks], axis=0, keepdims=True) * (0.25 / toks)
        )

    @pl.when(step == pl.num_programs(0) - 1)
    def _():
        mean = mean_ref[...]
        hi = mean.astype(bf16)
        lo = (mean - hi.astype(f32)).astype(bf16)
        wout = wout_ref[...]
        out_ref[...] = (
            jnp.dot(hi, wout, preferred_element_type=f32)
            + jnp.dot(lo, wout, preferred_element_type=f32)
            + tok_ref[...]
        )


def feed_forward(tokens, gain, weight_in, weight_out):
    rows, width = tokens.shape
    hidden = weight_in.shape[1]
    images = rows // 64
    block = 256
    return pl.pallas_call(
        ffn_kernel,
        grid=(rows // block,),
        in_specs=[
            pl.BlockSpec((block, width), lambda i: (i, 0)),
            pl.BlockSpec((1, width), lambda i: (0, 0)),
            pl.BlockSpec((width, hidden), lambda i: (0, 0)),
            pl.BlockSpec((hidden, width), lambda i: (0, 0)),
        ],
        out_specs=pl.BlockSpec((images, width), lambda i: (0, 0)),
        out_shape=jax.ShapeDtypeStruct((images, width), f32),
        scratch_shapes=[pltpu.VMEM((images, hidden), f32), pltpu.VMEM((images, width), f32)],
        compiler_params=params(),
        cost_estimate=pl.CostEstimate(
            flops=2 * rows * width * hidden, bytes_accessed=6 << 20, transcendentals=rows * hidden
        ),
        name="ffn",
    )(tokens, gain, weight_in, weight_out)


def unit_kernel(labels_ref, mine_ref, other_ref, gain_ref, send_ref, unit_ref, len_ref):
    images, width = mine_ref.shape
    pooled = mine_ref[...] + other_ref[...]
    embedding = layer_norm(pooled, gain_ref[...])
    length = jnp.sqrt(jnp.sum(embedding * embedding, axis=1, keepdims=True) + 1e-06)
    unit = (embedding / length).astype(bf16)
    row = lax.broadcasted_iota(jnp.int32, (images, lanes), 0)
    lane = lax.broadcasted_iota(jnp.int32, (images, lanes), 1)
    label = jnp.zeros((images, lanes), jnp.int32)
    for r in range(images):
        label = jnp.where(row == r, labels_ref[r], label)
    digits = jnp.where(
        lane == 0,
        label & 127,
        jnp.where(lane == 1, (label >> 7) & 127, jnp.where(lane == 2, label >> 14, 0)),
    )
    payload = jnp.concatenate([unit, digits.astype(f32).astype(bf16)], axis=1)
    for d in range(send_ref.shape[0]):
        send_ref[d] = payload
    unit_ref[...] = unit
    len_ref[...] = jnp.broadcast_to(length, (images, lanes))


def unit_rows_of(labels, mine, other, gain, homes):
    images, width = mine.shape
    return pl.pallas_call(
        unit_kernel,
        in_specs=[
            pl.BlockSpec(memory_space=pltpu.SMEM),
            pl.BlockSpec(memory_space=pltpu.VMEM),
            pl.BlockSpec(memory_space=pltpu.VMEM),
            pl.BlockSpec(memory_space=pltpu.VMEM),
        ],
        out_shape=(
            jax.ShapeDtypeStruct((homes, images, width + lanes), bf16),
            jax.ShapeDtypeStruct((images, width), bf16),
            jax.ShapeDtypeStruct((images, lanes), f32),
        ),
        compiler_params=params(),
        name="unit_rows",
    )(labels, mine, other, gain)


def centre_kernel(c_ref, after_ref, o_ref):
    wide = c_ref[...].astype(f32)
    o_ref[...] = (
        wide * lax.rsqrt(jnp.sum(wide * wide, axis=1, keepdims=True) + 1e-06)
    ).astype(bf16)


def unit_centres(centres, after):
    count, width = centres.shape
    block = 1024
    return pl.pallas_call(
        centre_kernel,
        grid=(count // block,),
        in_specs=[
            pl.BlockSpec((block, width), lambda i: (i, 0)),
            pl.BlockSpec(after.shape, lambda i: (0, 0)),
        ],
        out_specs=pl.BlockSpec((block, width), lambda i: (i, 0)),
        out_shape=jax.ShapeDtypeStruct((count, width), bf16),
        compiler_params=params(),
        cost_estimate=pl.CostEstimate(
            flops=4 * count * width, bytes_accessed=4 * count * width, transcendentals=count
        ),
        name="unit_centres",
    )(centres, after)


def digit_weights(shape, axis):
    at = lax.broadcasted_iota(jnp.int32, shape, axis)
    return jnp.where(
        at == 0, 1.0, jnp.where(at == 1, 128.0, jnp.where(at == 2, 16384.0, 0.0))
    ).astype(bf16)


def store_halves(core, width, keep_ref, send_ref, get):
    part = width // 4
    for group in range(2):
        keep_at = pl.multiple_of((2 * group + core) * part, part)
        send_at = pl.multiple_of((2 * group + 1 - core) * part, part)
        keep_ref[:, group * part : (group + 1) * part] = get(keep_at, part).astype(keep_ref.dtype)
        send_ref[:, group * part : (group + 1) * part] = get(send_at, part).astype(send_ref.dtype)


def target_kernel(where_ref, all_ref, centres_ref, keep_ref, send_ref, cos_ref, rows, found, lab, lab_s, sem, lab_sem):
    offset, core = where_ref[0], where_ref[1]
    images = all_ref.shape[0]
    count, width = centres_ref.shape
    weights = digit_weights((8, lanes), 1)
    row = lax.dot_general(
        weights, all_ref[:, width:], (((1,), (1,)), ((), ())), preferred_element_type=f32
    )
    lab[...] = row.astype(jnp.int32) - offset
    copy = pltpu.make_async_copy(lab, lab_s, lab_sem)
    copy.start()
    found[...] = jnp.zeros(found.shape, f32)
    copy.wait()

    def fetch(i):
        first = pl.multiple_of((lab_s[0, i] >> 4) << 4, 16)
        return pltpu.make_async_copy(centres_ref.at[pl.ds(first, 16), :], rows.at[i], sem)

    def local(i):
        at = lab_s[0, i]
        return jnp.logical_and(at >= 0, at < count)

    def start(i, c):
        @pl.when(local(i))
        def _():
            fetch(i).start()
        return c

    def finish(i, c):
        @pl.when(local(i))
        def _():
            fetch(i).wait()
        return c

    def take(i, c):
        @pl.when(local(i))
        def _():
            sub = lax.broadcasted_iota(jnp.int32, (16, width), 0)
            value = jnp.where(sub == (lab_s[0, i] & 15), rows[i].astype(f32), 0.0)
            found[pl.ds(i, 1), :] = jnp.sum(value, axis=0, keepdims=True)
        return c

    lax.fori_loop(0, images, start, 0, unroll=8)
    lax.fori_loop(0, images, finish, 0, unroll=8)
    lax.fori_loop(0, images, take, 0, unroll=8)
    cos = jnp.sum(found[...] * all_ref[:, :width].astype(f32), axis=1, keepdims=True)
    cos_ref[...] = jnp.broadcast_to(cos, cos_ref.shape)
    store_halves(core, width, keep_ref, send_ref, lambda at, n: found[:, pl.ds(at, n)])


def target_rows(where, gathered, centre_unit):
    images = gathered.shape[0]
    count, width = centre_unit.shape
    half = jax.ShapeDtypeStruct((images, width // 2), bf16)
    return pl.pallas_call(
        target_kernel,
        in_specs=[
            pl.BlockSpec(memory_space=pltpu.SMEM),
            pl.BlockSpec(memory_space=pltpu.VMEM),
            pl.BlockSpec(memory_space=pl.ANY),
        ],
        out_shape=(half, half, jax.ShapeDtypeStruct((images, lanes), f32)),
        scratch_shapes=[
            pltpu.VMEM((images, 16, width), bf16),
            pltpu.VMEM((images, width), f32),
            pltpu.VMEM((8, images), jnp.int32),
            pltpu.SMEM((8, images), jnp.int32),
            pltpu.SemaphoreType.DMA,
            pltpu.SemaphoreType.DMA,
        ],
        compiler_params=params(),
        cost_estimate=pl.CostEstimate(flops=1 << 20, bytes_accessed=8 << 20, transcendentals=0),
        name="target_rows",
    )(where, gathered, centre_unit)


def class_kernel(where_ref, all_ref, cos_ref, centres_ref, keep_ref, send_ref, acc, tot, lab):
    offset, core = where_ref[0], where_ref[1]
    step = pl.program_id(0)
    images = all_ref.shape[0]
    block, width = centres_ref.shape
    chunk = min(256, images)

    @pl.when(step == 0)
    def _():
        lab[...] = (
            jnp.dot(all_ref[:, width:], digit_weights((lanes, lanes), 0), preferred_element_type=f32)
        ).astype(jnp.int32) - offset
        acc[...] = jnp.zeros(acc.shape, f32)
        tot[...] = jnp.zeros(tot.shape, f32)

    base = step * block
    centres = centres_ref[...]
    for first in range(0, images, chunk):
        rows = slice(first, first + chunk)
        cosine = lax.dot_general(
            all_ref[rows, :width], centres, (((1,), (1,)), ((), ())), preferred_element_type=f32
        )
        local = lab[rows, :] - base
        lane = lax.broadcasted_iota(jnp.int32, (chunk, lanes), 1)
        parts = []
        total = tot[rows, :]
        for j in range(block // lanes):
            value = jnp.exp2(cosine[:, j * lanes : (j + 1) * lanes] * exp2_scale)
            value = jnp.where(local == lane + j * lanes, 0.0, value)
            total = total + value
            parts.append(value.astype(bf16))
        tot[rows, :] = total
        acc[rows, :] += jnp.dot(
            jnp.concatenate(parts, axis=1), centres, preferred_element_type=f32
        )

    @pl.when(step == pl.num_programs(0) - 1)
    def _():
        half = width // 2
        store_halves(core, width, keep_ref, send_ref, lambda at, n: acc[:, pl.ds(at, n)])
        total = jnp.sum(tot[...], axis=1, keepdims=True)
        inner = jnp.sum(acc[...] * all_ref[:, :width].astype(f32), axis=1, keepdims=True)
        extra = pack_extra((images, lanes), total, inner, cos_ref[...])
        keep_ref[:, half:] = extra
        send_ref[:, half:] = extra.astype(bf16)


def pack_extra(shape, total, inner, cos):
    lane = lax.broadcasted_iota(jnp.int32, shape, 1)
    out = jnp.zeros(shape, f32)
    for k, value in enumerate((total, inner, cos)):
        for j, piece in enumerate(split3(value)):
            out = jnp.where(lane == 3 * k + j, piece, out)
    return out


def unpack_extra(extra):
    values = []
    for k in range(3):
        values.append(
            extra[:, 3 * k : 3 * k + 1]
            + extra[:, 3 * k + 1 : 3 * k + 2]
            + extra[:, 3 * k + 2 : 3 * k + 3]
        )
    return values


def class_pass(where, gathered, cos, centre_unit):
    images = gathered.shape[0]
    count, width = centre_unit.shape
    block = 1024
    shape = (images, width // 2 + lanes)
    return pl.pallas_call(
        class_kernel,
        grid=(count // block,),
        in_specs=[
            pl.BlockSpec(memory_space=pltpu.SMEM),
            pl.BlockSpec(gathered.shape, lambda i: (0, 0)),
            pl.BlockSpec(cos.shape, lambda i: (0, 0)),
            pl.BlockSpec((block, width), lambda i: (i, 0)),
        ],
        out_specs=(
            pl.BlockSpec(shape, lambda i: (0, 0)),
            pl.BlockSpec(shape, lambda i: (0, 0)),
        ),
        out_shape=(jax.ShapeDtypeStruct(shape, f32), jax.ShapeDtypeStruct(shape, bf16)),
        scratch_shapes=[
            pltpu.VMEM((images, width), f32),
            pltpu.VMEM((images, lanes), f32),
            pltpu.VMEM((images, lanes), jnp.int32),
        ],
        compiler_params=params(),
        cost_estimate=pl.CostEstimate(
            flops=4 * images * count * width,
            bytes_accessed=2 * count * width,
            transcendentals=images * count,
        ),
        name="class_pass",
    )(where, gathered, cos, centre_unit)


def pair_kernel(keep_ref, got_ref, keep_row_ref, got_row_ref, out_ref):
    images = keep_ref.shape[0]
    half = keep_row_ref.shape[1]
    part = half // 2
    homes, own = out_ref.shape[0] // 2, out_ref.shape[1]
    summed = keep_ref[...] + got_ref[...].astype(f32)
    target = keep_row_ref[...] + got_row_ref[...]
    extra = pack_extra((images, lanes), *unpack_extra(summed[:, half:])).astype(bf16)
    for group in range(2):
        cols = slice(group * part, (group + 1) * part)
        at = slice(group * homes, (group + 1) * homes)
        out_ref[at, :, :part] = summed[:, cols].astype(bf16).reshape(homes, own, part)
        out_ref[at, :, part : 2 * part] = target[:, cols].reshape(homes, own, part)
        out_ref[at, :, 2 * part :] = extra.reshape(homes, own, lanes)


def pair_sum(keep, got, keep_rows, got_rows, homes):
    images = keep.shape[0]
    half = keep_rows.shape[1]
    return pl.pallas_call(
        pair_kernel,
        out_shape=jax.ShapeDtypeStruct((2 * homes, images // homes, half + lanes), bf16),
        compiler_params=params(),
        name="pair_sum",
    )(keep, got, keep_rows, got_rows)


def home_kernel(where_ref, got_ref, unit_ref, len_ref, loss_ref, grad_ref):
    column = where_ref[2]
    part = grad_ref.shape[1]
    summed = jnp.sum(got_ref[...].astype(f32), axis=0)
    gradient = summed[:, :part]
    target = summed[:, part : 2 * part]
    rest, inner, cos = unpack_extra(summed[:, 2 * part :])
    shifted, slope = arc_target(cos)
    own = jnp.exp(logit_scale * shifted)
    total = rest + own
    loss_ref[...] = jnp.broadcast_to(jnp.log(total) - logit_scale * shifted, loss_ref.shape)
    weight = (logit_scale * ((own / total - 1.0) * slope)).astype(bf16).astype(f32)
    scale = logit_scale / total
    dots = inner * scale + weight * cos
    unit = unit_ref[:, pl.ds(pl.multiple_of(column * part, part), part)].astype(f32)
    grad_ref[...] = (gradient * scale + weight * target - unit * dots) / len_ref[:, :1]


def home(where, got, unit, length):
    images = unit.shape[0]
    part = unit.shape[1] // 4
    return pl.pallas_call(
        home_kernel,
        in_specs=[
            pl.BlockSpec(memory_space=pltpu.SMEM),
            pl.BlockSpec(memory_space=pltpu.VMEM),
            pl.BlockSpec(memory_space=pltpu.VMEM),
            pl.BlockSpec(memory_space=pltpu.VMEM),
        ],
        out_shape=(
            jax.ShapeDtypeStruct((images, lanes), f32),
            jax.ShapeDtypeStruct((images, part), f32),
        ),
        compiler_params=params(),
        name="home",
    )(where, got, unit, length)


swap = [(0, 1), (1, 0)]


def shards(tokens, norm_gain, weight_in, weight_out, final_gain, centres, labels):
    images, tok_count, width = tokens.shape
    count = centres.shape[0]
    homes = lax.axis_size("dp")
    core = lax.axis_index("core")
    column = lax.axis_index("z_hi") * 2 + core
    offset = (column * homes + lax.axis_index("dp")) * count
    where = jnp.stack([offset, core, column]).astype(jnp.int32)

    partial = feed_forward(
        tokens.reshape(-1, width), norm_gain[None], weight_in, weight_out
    )
    partial = partial + lax.ppermute(partial, "core", swap)
    other = lax.ppermute(partial, "z_hi", swap)
    send, unit, length = unit_rows_of(labels, partial, other, final_gain[None], homes)
    gathered = lax.all_to_all(send, "dp", 0, 0, tiled=True).reshape(homes * images, -1)
    centre_unit = unit_centres(centres, length)
    keep_rows, send_rows, cos = target_rows(where, gathered, centre_unit)
    got_rows = lax.ppermute(send_rows, "core", swap)
    keep, give = class_pass(where, gathered, cos, centre_unit)
    got = lax.ppermute(give, "core", swap)
    paired = pair_sum(keep, got, keep_rows, got_rows, homes)
    arrived = lax.all_to_all(paired, ("z_hi", "dp"), 0, 0, tiled=True)
    loss, grad = home(where, arrived, unit, length)
    return (loss[:, 0], grad)


def solution(mesh):
    fine = Mesh(mesh.devices.reshape(2, 2, -1), ("z_hi", "core", "dp"))
    mp = ("z_hi", "core")
    return jax.shard_map(
        shards,
        mesh=fine,
        in_specs=(
            P("dp", None, None),
            P(),
            P(None, mp),
            P(mp, None),
            P(),
            P((*mp, "dp"), None),
            P("dp"),
        ),
        out_specs=(P("dp"), P("dp", mp)),
        check_vma=False,
    )
```

time: 541 us -> 133 us (0.25)
  waiting for transfers between devices: 347 us -> 8.98 us
  Pallas kernels: 0 us -> 74.9 us
  blocking collectives: 90.8 us -> 29.1 us
  matrix products: 55.8 us -> 0 us
  other arithmetic: 29.4 us -> 1.41 us
  between operations: 14.6 us -> 0.68 us
  starting transfers between devices: 0.16 us -> 12.7 us
    reduce_scatter x2 -> x0, waiting for transfers between devices: 185 us -> none  [the longest x1 161 us: shards(): lax.psum_scatter(grad_term, 'dp', scatter_dimension=0, tiled=True)]
    all_gather x1 -> x0, waiting for transfers between devices: 120 us -> none  [shards(): gathered = lax.all_gather(unit_rows, 'dp', axis=0, tiled=True)]
    pallas_call x0 -> x7, Pallas kernels: none -> 74.9 us  [the longest x1 25.7 us: class_pass(): pl.pallas_call(class_kernel, grid=(count // block,), in_specs=[pl.BlockSp...]
    psum x2 -> x0, blocking collectives: 71.8 us -> none  [the longest x1 64.5 us: shards(): lax.psum((jnp.sum(exponent, axis=1), jnp.where(is_owner, logit_scale * sh...]
    dot_general x3 -> x0, matrix products: 55.8 us -> none  [the longest x1 24.6 us: shards(): jnp.dot(weights, centre_unit, preferred_element_type=jnp.float32)]
    psum x1 -> x0, waiting for transfers between devices: 42.4 us -> none  [shards(): pooled = jnp.mean(tokens_wide, axis=1) + lax.psum(partial_value, 'mp')]
    all_to_all x0 -> x1, blocking collectives: none -> 29.1 us  [shards(): arrived = lax.all_to_all(paired, ('z_hi', 'dp'), 0, 0, tiled=True)]
    reduce_sum x8 -> x0, other arithmetic: 22.1 us -> none  [the longest x1 8.1 us: shards(): jnp.sum(exponent, axis=1)]
  transfers between devices with their start and end apart: 4 -> 5, of which waited for: 4 -> 4; matrix products, arithmetic and copies ran while one was open for 2% -> 0% of each run, Pallas kernels for 0% -> 12%
where the time goes in v1:
time: 133 us; the launch traced here: 132 us
  Pallas kernels  74.9 us (56%)
  blocking collectives  29.1 us (22%)
  starting transfers between devices  12.7 us (10%)
  waiting for transfers between devices  8.98 us (7%)
  local copies, waits for them, and re-layouts  4.04 us (3%)
  other arithmetic  1.41 us (1%)
    all_to_all x1, blocking collectives, shards(): arrived = lax.all_to_all(paired, ('z_hi', 'dp'), 0, 0, tiled=True)  29.1 us
    pallas_call x1, Pallas kernels, class_pass(): pl.pallas_call(class_kernel, grid=(count // block,), in_specs=[pl.BlockSp...  25.7 us
    pallas_call x1, Pallas kernels, target_rows(): pl.pallas_call(target_kernel, in_specs=[pl.BlockSpec(memory_space=pltpu.S...  16.9 us
    pallas_call x1, Pallas kernels, unit_centres(): pl.pallas_call(centre_kernel, grid=(count // block,), in_specs=[pl.BlockS...  15.4 us
    pallas_call x1, Pallas kernels, feed_forward(): pl.pallas_call(ffn_kernel, grid=(rows // block,), in_specs=[pl.BlockSpec(...  8.52 us
    all_to_all x1, starting transfers between devices, shards(): lax.all_to_all(send, 'dp', 0, 0, tiled=True).reshape(homes * images, -1)  8.15 us
    ppermute x1, starting transfers between devices, shards(): other = lax.ppermute(partial, 'z_hi', swap)  4.03 us
    pallas_call x1, Pallas kernels, pair_sum(): pl.pallas_call(pair_kernel, out_shape=jax.ShapeDtypeStruct((2 * homes, im...  3.64 us
  transfers between devices with their start and end apart: 5, of which 4 were waited for; matrix products, arithmetic and copies ran while one was open for 0% of the time, Pallas kernels for 12%

profile of v1, /device:TPU:0, one launch (start us, length us, event | category | flops | bytes accessed | tf_op | source)
XLA Modules:
  0.0 131.8 jit_solution(16454399294351658804)
XLA Ops:
  0.6 8.5 %ffn.1 = f32[16,1024]{1,0:T(8,128)} custom-call(bf16[1024,1024]{1,0:T(8,128)(2,1)} %bitcast.10, f32[1,1024]{1,0:T(1,128)} %bitcast.11, bf16[1024,1024]{1,0:T(8,128)(2,1)} %win_ref.1, bf16[1024,1024]{1,0:T(8,128)(2,1)} %wout_ref.1), custom_call_target="tpu_custom_call" | custom-call | flops 2147483648 | bytes 6291456 | tf_op jit(solution)/shard_map/ffn/pallas_call | solution.py:85
  9.2 1.5 %collective-permute-done = f32[16,1024]{1,0:T(8,128)S(1)} collective-permute-done((f32[16,1024]{1,0:T(8,128)}, f32[16,1024]{1,0:T(8,128)S(1)}, u32[]{:S(2)}, u32[]{:S(2)}) %collective-permute-start) | collective-permute-done | bytes 65568 | tf_op jit(solution)/shard_map/ppermute | solution.py:448
  10.6 0.9 add.11.mine_ref
  11.5 4.0 %collective-permute-start.1 = (f32[16,1024]{1,0:T(8,128)S(1)}, f32[16,1024]{1,0:T(8,128)S(1)}, u32[]{:S(2)}, u32[]{:S(2)}) collective-permute-start(f32[16,1024]{1,0:T(8,128)S(1)} %add.11.mine_ref), channel_id=1, source_target_pairs={{0,64},{64,0},{1,65},{65,1},{2,66},{66,2},{3,67},{67,3},{4,68},{68... | collective-permute-start | bytes 196616 | tf_op jit(solution)/shard_map/ppermute | solution.py:449
  15.5 2.4 %collective-permute-done.1.other_ref = f32[16,1024]{1,0:T(8,128)S(1)} collective-permute-done((f32[16,1024]{1,0:T(8,128)S(1)}, f32[16,1024]{1,0:T(8,128)S(1)}, u32[]{:S(2)}, u32[]{:S(2)}) %collective-permute-start.1) | collective-permute-done | bytes 65568 | tf_op jit(solution)/shard_map/ppermute | solution.py:449
  17.9 0.6 copy-done.4
  18.5 2.3 %unit_rows.1 = (bf16[32,16,1152]{2,1,0:T(8,128)(2,1)}, bf16[16,1024]{1,0:T(8,128)(2,1)}, f32[16,128]{1,0:T(8,128)}) custom-call(s32[16]{0:T(128)} %labels_ref.1, f32[16,1024]{1,0:T(8,128)} %copy-done.3, f32[16,1024]{1,0:T(8,128)} %copy-done.4, f32[1,1024]{1,0:T(1,128)} %bitcast.9), custom_call_target="tpu_custom_call" | custom-call | tf_op jit(solution)/shard_map/unit_rows/pallas_call | solution.py:130
  20.8 8.2 %all-to-all-start = ((bf16[32,16,1152]{2,1,0:T(8,128)(2,1)}), bf16[32,16,1152]{2,1,0:T(8,128)(2,1)S(1)}, u32[]{:S(2)}, u32[]{:S(2)}) async-start(bf16[32,16,1152]{2,1,0:T(8,128)(2,1)} %get-tuple-element.12), calls=%async_computation | async-start | bytes 2359296 | tf_op jit(solution)/shard_map/all_to_all | solution.py:451
  29.0 0.6 pad_add_fusion.where_ref
  29.5 15.4 %unit_centres.1.centres_ref = bf16[8192,1024]{1,0:T(8,128)(2,1)} custom-call(bf16[8192,1024]{1,0:T(8,128)(2,1)} %c_ref.1, f32[16,128]{1,0:T(8,128)} %get-tuple-element.13.after_ref.len_ref), custom_call_target="tpu_custom_call" | custom-call | flops 33554432 | bytes 33554432 | tf_op jit(solution)/shard_map/unit_centres/pallas_call | solution.py:158
  45.0 2.8 %all-to-all-done = bf16[32,16,1152]{2,1,0:T(8,128)(2,1)S(1)} async-done(((bf16[32,16,1152]{2,1,0:T(8,128)(2,1)}), bf16[32,16,1152]{2,1,0:T(8,128)(2,1)S(1)}, u32[]{:S(2)}, u32[]{:S(2)}) %all-to-all-start) | async-done | bytes 1179680 | tf_op jit(solution)/shard_map/all_to_all | solution.py:451
  47.8 1.0 copy-done
  48.8 16.9 %target_rows.1 = (bf16[512,512]{1,0:T(8,128)(2,1)}, bf16[512,512]{1,0:T(8,128)(2,1)}, f32[512,128]{1,0:T(8,128)}) custom-call(s32[3]{0:T(128)} %pad_add_fusion.where_ref, bf16[512,1152]{1,0:T(8,128)(2,1)} %bitcast.7, bf16[8192,1024]{1,0:T(8,128)(2,1)} %unit_centres.1.centres_ref), custom_call_target="tpu_custom_call" | custom-call | flops 1048576 | bytes 8388608 | tf_op jit(solution)/shard_map/target_rows/pallas_call | solution.py:245
  65.7 25.7 %class_pass.1 = (f32[512,640]{1,0:T(8,128)}, bf16[512,640]{1,0:T(8,128)(2,1)}) custom-call(s32[3]{0:T(128)} %pad_add_fusion.where_ref, bf16[512,1152]{1,0:T(8,128)(2,1)} %bitcast.8, f32[512,128]{1,0:T(8,128)} %get-tuple-element.14.cos_ref, bf16[8192,1024]{1,0:T(8,128)(2,1)} %unit_centres.1.centres_ref), custom_call_target="tpu_custom_call" | custom-call | flops 17179869184 | bytes 16777216 | tf_op jit(solution)/shard_map/class_pass/pallas_call | solution.py:339
  91.4 0.0 collective-permute-start.2
  91.4 0.5 collective-permute-start.3
  91.9 2.3 %collective-permute-done.3.got_row_ref = bf16[512,512]{1,0:T(8,128)(2,1)S(1)} collective-permute-done((bf16[512,512]{1,0:T(8,128)(2,1)S(1)}, bf16[512,512]{1,0:T(8,128)(2,1)S(1)}, u32[]{:S(2)}, u32[]{:S(2)}) %collective-permute-start.3) | collective-permute-done | bytes 524320 | tf_op jit(solution)/shard_map/ppermute | solution.py:454
  94.3 0.0 collective-permute-done.2.got_ref
  94.3 0.8 copy-done.2
  95.1 0.3 copy-done.1
  95.4 3.6 %pair_sum.1 = bf16[64,16,640]{2,1,0:T(8,128)(2,1)} custom-call(f32[512,640]{1,0:T(8,128)} %get-tuple-element.15.keep_ref, bf16[512,640]{1,0:T(8,128)(2,1)} %copy-done.1, bf16[512,512]{1,0:T(8,128)(2,1)} %get-tuple-element.17.keep_row_ref, bf16[512,512]{1,0:T(8,128)(2,1)} %copy-done.2), custom_call_target="tpu_custom_call" | custom-call | tf_op jit(solution)/shard_map/pair_sum/pallas_call | solution.py:387
  99.0 29.1 %all_to_all.10.got_ref = bf16[64,16,640]{2,1,0:T(8,128)(2,1)} all-to-all(bf16[64,16,640]{2,1,0:T(8,128)(2,1)} %pair_sum.1), channel_id=1, replica_groups=mesh['z_hi'=2,'core'=2,'dp'=32] {'z_hi','dp'}, dimensions={0} | all-to-all | bytes 2621440 | tf_op jit(solution)/shard_map/all_to_all | solution.py:458
  128.1 2.4 %home.1 = (f32[16,128]{1,0:T(8,128)}, f32[16,256]{1,0:T(8,128)}) custom-call(s32[3]{0:T(128)} %pad_add_fusion.where_ref, bf16[64,16,640]{2,1,0:T(8,128)(2,1)} %all_to_all.10.got_ref, bf16[16,1024]{1,0:T(8,128)(2,1)} %get-tuple-element.19.unit_ref, f32[16,128]{1,0:T(8,128)} %get-tuple-element.13.after_ref.len_ref), custom_call_target="tpu_custom_call" | custom-call | tf_op jit(solution)/shard_map/home/pallas_call | solution.py:416
  130.5 1.3 %slice_reduce_fusion = f32[16]{0:T(128)} fusion(f32[16,128]{1,0:T(8,128)} %get-tuple-element.20), kind=kLoop, calls=%fused_computation | loop fusion | bytes 128 | tf_op jit(solution)/shard_map/slice | solution.py:460
  (9 shorter events, 0.0 us)
Async XLA Ops:
  9.1 1.5 %collective-permute-start = (f32[16,1024]{1,0:T(8,128)}, f32[16,1024]{1,0:T(8,128)S(1)}, u32[]{:S(2)}, u32[]{:S(2)}) collective-permute-start(f32[16,1024]{1,0:T(8,128)} %ffn.1), channel_id=1, source_target_pairs={{0,32},{32,0},{1,33},{33,1},{2,34},{34,2},{3,35},{35,3},{4,36},{36... | collective-permute-start | bytes 196616 | tf_op jit(solution)/shard_map/ppermute | solution.py:448
  11.5 6.5 %copy-start.3 = (f32[16,1024]{1,0:T(8,128)}, f32[16,1024]{1,0:T(8,128)S(1)}, u32[]{:S(2)}) copy-start(f32[16,1024]{1,0:T(8,128)S(1)} %add.11.mine_ref) | copy-start | bytes 196612
  11.5 6.4 %collective-permute-start.1 = (f32[16,1024]{1,0:T(8,128)S(1)}, f32[16,1024]{1,0:T(8,128)S(1)}, u32[]{:S(2)}, u32[]{:S(2)}) collective-permute-start(f32[16,1024]{1,0:T(8,128)S(1)} %add.11.mine_ref), channel_id=1, source_target_pairs={{0,64},{64,0},{1,65},{65,1},{2,66},{66,2},{3,67},{67,3},{4,68},{68... | collective-permute-start | bytes 196616 | tf_op jit(solution)/shard_map/ppermute | solution.py:449
  17.9 0.6 copy-start.4
  20.8 26.9 %all-to-all-start = ((bf16[32,16,1152]{2,1,0:T(8,128)(2,1)}), bf16[32,16,1152]{2,1,0:T(8,128)(2,1)S(1)}, u32[]{:S(2)}, u32[]{:S(2)}) async-start(bf16[32,16,1152]{2,1,0:T(8,128)(2,1)} %get-tuple-element.12), calls=%async_computation | async-start | bytes 2359296 | tf_op jit(solution)/shard_map/all_to_all | solution.py:451
  47.8 1.0 copy-start
  65.7 25.7 %copy-start.5 = (bf16[512,512]{1,0:T(8,128)(2,1)S(1)}, bf16[512,512]{1,0:T(8,128)(2,1)}, u32[]{:S(2)}) copy-start(bf16[512,512]{1,0:T(8,128)(2,1)} %get-tuple-element.18) | copy-start | bytes 1572868
  91.4 2.9 %collective-permute-start.2 = (bf16[512,640]{1,0:T(8,128)(2,1)}, bf16[512,640]{1,0:T(8,128)(2,1)S(1)}, u32[]{:S(2)}, u32[]{:S(2)}) collective-permute-start(bf16[512,640]{1,0:T(8,128)(2,1)} %get-tuple-element.16), channel_id=1, source_target_pairs={{0,32},{32,0},{1,33},{33,1},{2,34},{34,2},{3,35},{35,3},{4,36},{36... | collective-permute-start | bytes 1966088 | tf_op jit(solution)/shard_map/ppermute | solution.py:456
  91.4 2.8 %collective-permute-start.3 = (bf16[512,512]{1,0:T(8,128)(2,1)S(1)}, bf16[512,512]{1,0:T(8,128)(2,1)S(1)}, u32[]{:S(2)}, u32[]{:S(2)}) collective-permute-start(bf16[512,512]{1,0:T(8,128)(2,1)S(1)} %copy-done.5), channel_id=1, source_target_pairs={{0,32},{32,0},{1,33},{33,1},{2,34},{34,2},{3,35},{35,3},{4,36},{36... | collective-permute-start | bytes 1572872 | tf_op jit(solution)/shard_map/ppermute | solution.py:454
  94.3 0.8 copy-start.2
  94.3 1.1 copy-start.1

commit v2 on v0

v2 whole, which is shorter than its diff:
```python
import math

import jax
import jax.numpy as jnp
from jax import lax
from jax.experimental import pallas as pl
from jax.experimental.pallas import tpu as pltpu
from jax.sharding import Mesh, PartitionSpec as P

logit_scale = 64.0
angle_margin = 0.5
exp2_scale = logit_scale / math.log(2.0)
lanes = 128
digits = 3
pieces = 8
f32 = jnp.float32
bf16 = jnp.bfloat16


def params(mebibytes):
    return pltpu.CompilerParams(vmem_limit_bytes=mebibytes * 1024 * 1024)


def arc_target(target_cos):
    target_sine = jnp.sqrt(jnp.maximum(1.0 - target_cos * target_cos, 0.01))
    inside = target_cos > -math.cos(angle_margin)
    shifted = jnp.where(
        inside,
        target_cos * math.cos(angle_margin) - target_sine * math.sin(angle_margin),
        target_cos - angle_margin * math.sin(angle_margin),
    )
    margin_slope = jnp.where(
        inside, math.cos(angle_margin) + math.sin(angle_margin) * target_cos / target_sine, 1.0
    )
    return (shifted, margin_slope)


def layer_norm(values, gain_vec):
    average = jnp.mean(values, axis=-1, keepdims=True)
    centred = values - average
    variance = jnp.mean(centred * centred, axis=-1, keepdims=True)
    return centred * lax.rsqrt(variance + 1e-06) * gain_vec


def split3(value):
    hi = value.astype(bf16).astype(f32)
    mid = (value - hi).astype(bf16).astype(f32)
    return hi, mid, value - hi - mid


def ffn_kernel(tokens_ref, gain_ref, win_ref, wout_ref, out_ref, mean_ref, tok_ref):
    step = pl.program_id(0)
    block, width = tokens_ref.shape
    toks = 64
    per = block // toks
    wide = tokens_ref[...].astype(f32)
    normed = layer_norm(wide, gain_ref[...]).astype(bf16)
    pre = jnp.dot(normed, win_ref[...], preferred_element_type=f32)
    hidden = (0.5 * pre * (1.0 + lax.erf(pre * math.sqrt(0.5)))).astype(bf16).astype(f32)
    for k in range(per):
        mean_ref[pl.ds(step * per + k, 1), :] = (
            jnp.sum(hidden[k * toks : (k + 1) * toks], axis=0, keepdims=True) * (1.0 / toks)
        )
        tok_ref[pl.ds(step * per + k, 1), :] = (
            jnp.sum(wide[k * toks : (k + 1) * toks], axis=0, keepdims=True) * (0.25 / toks)
        )

    @pl.when(step == pl.num_programs(0) - 1)
    def _():
        mean = mean_ref[...]
        hi = mean.astype(bf16)
        lo = (mean - hi.astype(f32)).astype(bf16)
        both = jnp.dot(
            jnp.concatenate([hi, lo], axis=0), wout_ref[...], preferred_element_type=f32
        )
        images = mean.shape[0]
        out_ref[...] = both[:images] + both[images:] + tok_ref[...]


def feed_forward(tokens, gain, weight_in, weight_out):
    rows, width = tokens.shape
    hidden = weight_in.shape[1]
    images = rows // 64
    block = 256
    return pl.pallas_call(
        ffn_kernel,
        grid=(rows // block,),
        in_specs=[
            pl.BlockSpec((block, width), lambda i: (i, 0)),
            pl.BlockSpec((1, width), lambda i: (0, 0)),
            pl.BlockSpec((width, hidden), lambda i: (0, 0)),
            pl.BlockSpec((hidden, width), lambda i: (0, 0)),
        ],
        out_specs=pl.BlockSpec((images, width), lambda i: (0, 0)),
        out_shape=jax.ShapeDtypeStruct((images, width), f32),
        scratch_shapes=[pltpu.VMEM((images, hidden), f32), pltpu.VMEM((images, width), f32)],
        compiler_params=params(56),
        cost_estimate=pl.CostEstimate(
            flops=2 * rows * width * hidden, bytes_accessed=6 << 20, transcendentals=rows * hidden
        ),
        name="ffn",
    )(tokens, gain, weight_in, weight_out)


def unit_kernel(where_ref, labels_ref, mine_ref, other_ref, gain_ref, send_ref, unit_ref, len_ref):
    images, width = mine_ref.shape
    pooled = mine_ref[...] + other_ref[...]
    embedding = layer_norm(pooled, gain_ref[...])
    length = jnp.sqrt(jnp.sum(embedding * embedding, axis=1, keepdims=True) + 1e-06)
    unit = (embedding / length).astype(bf16).astype(f32)
    half = images // 2
    row = lax.broadcasted_iota(jnp.int32, (half, lanes), 0)
    lane = lax.broadcasted_iota(jnp.int32, (half, lanes), 1)
    label = jnp.zeros((half, lanes), jnp.int32)
    for h in range(2):
        for r in range(half):
            here = jnp.logical_and(row == r, lane // digits == h)
            label = jnp.where(here, labels_ref[h * half + r], label)
    place = lane % digits
    coded = jnp.where(
        place == 0, label & 127, jnp.where(place == 1, (label >> 7) & 127, label >> 14)
    )
    payload = jnp.concatenate([unit[:half], unit[half:], coded.astype(f32)], axis=1)
    payload = jnp.concatenate([payload, payload], axis=0).astype(bf16)
    for d in range(send_ref.shape[0] // images):
        send_ref[d * images : (d + 1) * images, :] = payload
    unit_ref[...] = unit
    len_ref[...] = jnp.broadcast_to(length, (images, lanes))


def unit_rows_of(where, labels, mine, other, gain, homes):
    images, width = mine.shape
    return pl.pallas_call(
        unit_kernel,
        in_specs=[
            pl.BlockSpec(memory_space=pltpu.SMEM),
            pl.BlockSpec(memory_space=pltpu.SMEM),
            pl.BlockSpec(memory_space=pltpu.VMEM),
            pl.BlockSpec(memory_space=pltpu.VMEM),
            pl.BlockSpec(memory_space=pltpu.VMEM),
        ],
        out_shape=(
            jax.ShapeDtypeStruct((homes * images // 2, 2 * width + lanes), bf16),
            jax.ShapeDtypeStruct((images, width), f32),
            jax.ShapeDtypeStruct((images, lanes), f32),
        ),
        compiler_params=params(8),
        name="unit_rows",
    )(where, labels, mine, other, gain)


def digit_weights(shape, axis, h):
    at = lax.broadcasted_iota(jnp.int32, shape, axis) - h * digits
    return jnp.where(
        at == 0, 1.0, jnp.where(at == 1, 128.0, jnp.where(at == 2, 16384.0, 0.0))
    ).astype(bf16)


group_size = 16


def class_kernel(
    where_ref,
    all_ref,
    centres_ref,
    keep_ref,
    keep_row_ref,
    send_ref,
    held,
    unit,
    acc,
    tot,
    cos_row,
    lab,
    lab_s,
    found_s,
    lab_sem,
    sems,
):
    offset, core = where_ref[0], where_ref[1]
    rows = all_ref.shape[0]
    images = 2 * rows
    count, width = centres_ref.shape
    block = count // pieces
    half, part = width // 2, width // 4
    groups = images // group_size

    def fetch(i):
        at = pl.ds(pl.multiple_of(i * block, block), block)
        return pltpu.make_async_copy(centres_ref.at[at, :], held.at[at, :], sems.at[i])

    for i in range(pieces):
        fetch(i).start()

    coded = all_ref[:, 2 * width :]
    turned = (((1,), (1,)), ((), ()))
    for h in range(2):
        unit[h * rows : (h + 1) * rows, :] = all_ref[:, h * width : (h + 1) * width]
        lab[:, h * rows : (h + 1) * rows] = lax.dot_general(
            digit_weights((8, lanes), 1, h), coded, turned, preferred_element_type=f32
        ).astype(jnp.int32) - offset
    row = lab[:, :images]
    member = lax.broadcasted_iota(jnp.int32, (images, lanes), 0) // group_size
    member = (member == lax.broadcasted_iota(jnp.int32, (images, lanes), 1)).astype(bf16)
    inside = jnp.logical_and(row >= 0, row < count).astype(f32).astype(bf16)
    lab[:, images:] = jnp.dot(inside, member, preferred_element_type=f32).astype(jnp.int32)
    copy = pltpu.make_async_copy(lab, lab_s, lab_sem)
    copy.start()
    local = jnp.concatenate(
        [
            jnp.dot(coded, digit_weights((lanes, lanes), 0, h), preferred_element_type=f32)
            for h in range(2)
        ],
        axis=0,
    ).astype(jnp.int32) - offset
    acc[...] = jnp.zeros(acc.shape, f32)
    tot[...] = jnp.zeros(tot.shape, f32)
    cos_row[...] = jnp.zeros(cos_row.shape, f32)
    keep_row_ref[...] = jnp.zeros(keep_row_ref.shape, bf16)
    send_ref[:, width : 2 * width] = jnp.zeros((rows, width), bf16)
    copy.wait()
    found_s[images] = 0

    def look(g, c):
        @pl.when(lab_s[0, images + g] > 0)
        def _():
            for k in range(group_size):
                i = g * group_size + k
                at = lab_s[0, i]

                @pl.when(jnp.logical_and(at >= 0, at < count))
                def _():
                    n = found_s[images]
                    found_s[n] = i
                    found_s[images] = n + 1

        return c

    lax.fori_loop(0, groups, look, 0)

    diagonal = lax.broadcasted_iota(jnp.int32, (lanes, lanes), 0) == lax.broadcasted_iota(
        jnp.int32, (lanes, lanes), 1
    )

    def step(t, c):
        base = pl.multiple_of(t * block, block)
        fetch(t).wait()
        centres = held[pl.ds(base, block), :]
        cosine = lax.dot_general(unit[...], centres, turned, preferred_element_type=f32)
        lane = lax.broadcasted_iota(jnp.int32, (images, lanes), 1) + base
        parts = []
        total = tot[...]
        for j in range(block // lanes):
            wide = held[pl.ds(base + j * lanes, lanes), :].astype(f32)
            square = jnp.sum(wide * wide, axis=1, keepdims=True)
            square = jnp.sum(jnp.where(diagonal, square, 0.0), axis=0, keepdims=True)
            inverse = lax.rsqrt(square + 1e-06)
            value = jnp.exp2(cosine[:, j * lanes : (j + 1) * lanes] * (inverse * exp2_scale))
            value = jnp.where(local == lane + j * lanes, 0.0, value)
            total = total + value
            parts.append((value * inverse).astype(bf16))
        tot[...] = total
        acc[...] += jnp.dot(jnp.concatenate(parts, axis=1), centres, preferred_element_type=f32)
        return c

    lax.fori_loop(0, pieces, step, 0)

    sub = lax.broadcasted_iota(jnp.int32, (16, width), 0)

    def take(k, c):
        i = found_s[k]
        at = lab_s[0, i]
        raw = held[pl.ds(pl.multiple_of((at >> 4) << 4, 16), 16), :].astype(f32)
        raw = jnp.sum(jnp.where(sub == (at & 15), raw, 0.0), axis=0, keepdims=True)
        found = raw * lax.rsqrt(jnp.sum(raw * raw, axis=1, keepdims=True) + 1e-06)
        found = found.astype(bf16).astype(f32)
        mine = sub == (i & 15)
        first = pl.multiple_of((i >> 4) << 4, 16)
        image = unit[pl.ds(first, 16), :].astype(f32)
        cos = jnp.sum(jnp.where(mine, image * found, 0.0), axis=1, keepdims=True)
        cos_row[pl.ds(first, 16), :] = jnp.where(
            mine[:, :lanes], cos, cos_row[pl.ds(first, 16), :]
        )
        even = jnp.concatenate([found[:, :part], found[:, half : half + part]], axis=1)
        odd = jnp.concatenate([found[:, part:half], found[:, half + part :]], axis=1)
        kept = jnp.where(core == 0, even, odd)
        sent = jnp.where(core == 0, odd, even)
        for h in range(2):

            @pl.when((i >= rows) == (h == 1))
            def _():
                here = pl.ds(pl.multiple_of(first - h * rows, 16), 16)
                for ref, start, value in ((keep_row_ref, 0, kept), (send_ref, width, sent)):
                    cols = slice(start + h * half, start + (h + 1) * half)
                    ref[here, cols] = jnp.where(
                        mine[:, :half], value, ref[here, cols].astype(f32)
                    ).astype(bf16)

        return c

    lax.fori_loop(0, found_s[images], take, 0)

    extras = []
    for h in range(2):
        at = slice(h * rows, (h + 1) * rows)
        for group in range(2):
            cols = slice(h * half + group * part, h * half + (group + 1) * part)
            keep_at = pl.multiple_of((2 * group + core) * part, part)
            send_at = pl.multiple_of((2 * group + 1 - core) * part, part)
            keep_ref[:, cols] = acc[at, pl.ds(keep_at, part)]
            send_ref[:, cols] = acc[at, pl.ds(send_at, part)].astype(bf16)
        total = jnp.sum(tot[at, :], axis=1, keepdims=True)
        inner = jnp.sum(acc[at, :] * unit[at, :].astype(f32), axis=1, keepdims=True)
        extras.append((total, inner, cos_row[at, :1]))
    extra = pack_extra(extras)
    keep_ref[:, width:] = extra
    send_ref[:, 2 * width :] = extra.astype(bf16)


def pack_extra(halves):
    shape = (halves[0][0].shape[0], lanes)
    lane = lax.broadcasted_iota(jnp.int32, shape, 1)
    out = jnp.zeros(shape, f32)
    k = 0
    for values in halves:
        for value in values:
            for piece in split3(value):
                out = jnp.where(lane == k, piece, out)
                k += 1
    return out


def unpack_extra(extra):
    halves = []
    for h in range(2):
        values = []
        for k in range(3 * h, 3 * h + 3):
            values.append(
                extra[:, 3 * k : 3 * k + 1]
                + extra[:, 3 * k + 1 : 3 * k + 2]
                + extra[:, 3 * k + 2 : 3 * k + 3]
            )
        halves.append(values)
    return halves


def class_pass(where, gathered, centres):
    rows = gathered.shape[0]
    images = 2 * rows
    count, width = centres.shape
    return pl.pallas_call(
        class_kernel,
        in_specs=[
            pl.BlockSpec(memory_space=pltpu.SMEM),
            pl.BlockSpec(memory_space=pltpu.VMEM),
            pl.BlockSpec(memory_space=pltpu.HBM),
        ],
        out_shape=(
            jax.ShapeDtypeStruct((rows, width + lanes), f32),
            jax.ShapeDtypeStruct((rows, width), bf16),
            jax.ShapeDtypeStruct((rows, 2 * width + lanes), bf16),
        ),
        scratch_shapes=[
            pltpu.VMEM((count, width), bf16),
            pltpu.VMEM((images, width), bf16),
            pltpu.VMEM((images, width), f32),
            pltpu.VMEM((images, lanes), f32),
            pltpu.VMEM((images, lanes), f32),
            pltpu.VMEM((8, images + lanes), jnp.int32),
            pltpu.SMEM((8, images + lanes), jnp.int32),
            pltpu.SMEM((images + 1,), jnp.int32),
            pltpu.SemaphoreType.DMA,
            pltpu.SemaphoreType.DMA((pieces,)),
        ],
        compiler_params=params(48),
        cost_estimate=pl.CostEstimate(
            flops=4 * images * count * width,
            bytes_accessed=2 * count * width,
            transcendentals=images * count,
        ),
        name="class_pass",
    )(where, gathered, centres)


def pair_kernel(keep_ref, keep_row_ref, got_ref, out_ref):
    rows, width = keep_row_ref.shape
    half, part = width // 2, width // 4
    summed = keep_ref[...] + jnp.concatenate(
        [got_ref[:, :width].astype(f32), got_ref[:, 2 * width :].astype(f32)], axis=1
    )
    target = keep_row_ref[...] + got_ref[:, width : 2 * width]
    extra = pack_extra(unpack_extra(summed[:, width:])).astype(bf16)
    for group in range(2):
        at = slice(group * rows, (group + 1) * rows)
        for h in range(2):
            cols = slice(h * half + group * part, h * half + (group + 1) * part)
            out_ref[at, h * part : (h + 1) * part] = summed[:, cols].astype(bf16)
            out_ref[at, half + h * part : half + (h + 1) * part] = target[:, cols]
        out_ref[at, width:] = extra


def pair_sum(keep, keep_rows, got):
    rows, width = keep_rows.shape
    return pl.pallas_call(
        pair_kernel,
        out_shape=jax.ShapeDtypeStruct((2 * rows, width + lanes), bf16),
        compiler_params=params(12),
        name="pair_sum",
    )(keep, keep_rows, got)


def home_kernel(where_ref, got_ref, unit_ref, len_ref, loss_ref, grad_ref):
    column = where_ref[2]
    images, part = grad_ref.shape
    half = images // 2
    summed = jnp.zeros((images, got_ref.shape[1]), f32)
    for k in range(0, got_ref.shape[0], images):
        summed = summed + got_ref[k : k + images, :].astype(f32)
    summed = summed[:half] + summed[half:]
    row = lax.broadcasted_iota(jnp.int32, (half, images), 0)
    lane = lax.broadcasted_iota(jnp.int32, (half, images), 1)
    loss_row = jnp.zeros((1, images), f32)
    for h, (rest, inner, cos) in enumerate(unpack_extra(summed[:, 4 * part :])):
        at = slice(h * half, (h + 1) * half)
        gradient = summed[:, h * part : (h + 1) * part]
        target = summed[:, (2 + h) * part : (3 + h) * part]
        shifted, slope = arc_target(cos)
        own = jnp.exp(logit_scale * shifted)
        total = rest + own
        loss = jnp.log(total) - logit_scale * shifted
        loss_row += jnp.sum(jnp.where(lane == row + h * half, loss, 0.0), axis=0, keepdims=True)
        weight = (logit_scale * ((own / total - 1.0) * slope)).astype(bf16).astype(f32)
        scale = logit_scale / total
        dots = inner * scale + weight * cos
        unit = unit_ref[at, pl.ds(pl.multiple_of(column * part, part), part)]
        grad_ref[at, :] = (gradient * scale + weight * target - unit * dots) / len_ref[at, :1]
    loss_ref[...] = loss_row


def home(where, got, unit, length):
    images = unit.shape[0]
    part = unit.shape[1] // 4
    return pl.pallas_call(
        home_kernel,
        in_specs=[
            pl.BlockSpec(memory_space=pltpu.SMEM),
            pl.BlockSpec(memory_space=pltpu.VMEM),
            pl.BlockSpec(memory_space=pltpu.VMEM),
            pl.BlockSpec(memory_space=pltpu.VMEM),
        ],
        out_shape=(
            jax.ShapeDtypeStruct((1, images), f32),
            jax.ShapeDtypeStruct((images, part), f32),
        ),
        compiler_params=params(12),
        name="home",
    )(where, got, unit, length)


swap = [(0, 1), (1, 0)]


def shards(tokens, norm_gain, weight_in, weight_out, final_gain, centres, labels):
    images, tok_count, width = tokens.shape
    count = centres.shape[0]
    homes = lax.axis_size("dp")
    core = lax.axis_index("core")
    column = lax.axis_index("z_hi") * 2 + core
    offset = (column * homes + lax.axis_index("dp")) * count
    where = jnp.stack([offset, core, column]).astype(jnp.int32)

    partial = feed_forward(
        tokens.reshape(-1, width), norm_gain[None], weight_in, weight_out
    )
    partial = partial + lax.ppermute(partial, "core", swap)
    other = lax.ppermute(partial, "z_hi", swap)
    send, unit, length = unit_rows_of(where, labels, partial, other, final_gain[None], homes)
    gathered = lax.all_to_all(send, "dp", 0, 0, tiled=True)
    keep, keep_rows, give = class_pass(where, gathered, centres)
    got = lax.ppermute(give, "core", swap)
    paired = pair_sum(keep, keep_rows, got)
    arrived = lax.all_to_all(paired, ("z_hi", "dp"), 0, 0, tiled=True)
    loss, grad = home(where, arrived, unit, length)
    return (loss[0], grad)


def solution(mesh):
    fine = Mesh(mesh.devices.reshape(2, 2, -1), ("z_hi", "core", "dp"))
    mp = ("z_hi", "core")
    return jax.shard_map(
        shards,
        mesh=fine,
        in_specs=(
            P("dp", None, None),
            P(),
            P(None, mp),
            P(mp, None),
            P(),
            P((*mp, "dp"), None),
            P("dp"),
        ),
        out_specs=(P("dp"), P("dp", mp)),
        check_vma=False,
    )
```

time: 541 us -> 102 us (0.19)
  waiting for transfers between devices: 347 us -> 6.54 us
  matrix products: 55.8 us -> 0 us
  blocking collectives: 90.8 us -> 52 us
  Pallas kernels: 0 us -> 37.1 us
  other arithmetic: 29.4 us -> 0.93 us
  between operations: 14.6 us -> 0.68 us
    reduce_scatter x2 -> x0, waiting for transfers between devices: 185 us -> none  [the longest x1 161 us: shards(): lax.psum_scatter(grad_term, 'dp', scatter_dimension=0, tiled=True)]
    all_gather x1 -> x0, waiting for transfers between devices: 120 us -> none  [shards(): gathered = lax.all_gather(unit_rows, 'dp', axis=0, tiled=True)]
    psum x2 -> x0, blocking collectives: 71.8 us -> none  [the longest x1 64.5 us: shards(): lax.psum((jnp.sum(exponent, axis=1), jnp.where(is_owner, logit_scale * sh...]
    dot_general x3 -> x0, matrix products: 55.8 us -> none  [the longest x1 24.6 us: shards(): jnp.dot(weights, centre_unit, preferred_element_type=jnp.float32)]
    all_to_all x0 -> x2, blocking collectives: none -> 52 us  [the longest x1 26.4 us: shards(): arrived = lax.all_to_all(paired, ('z_hi', 'dp'), 0, 0, tiled=True)]
    psum x1 -> x0, waiting for transfers between devices: 42.4 us -> none  [shards(): pooled = jnp.mean(tokens_wide, axis=1) + lax.psum(partial_value, 'mp')]
    pallas_call x0 -> x5, Pallas kernels: none -> 37.1 us  [the longest x1 25.6 us: class_pass(): pl.pallas_call(class_kernel, in_specs=[pl.BlockSpec(memory_space=pltpu.SM...]
    reduce_sum x8 -> x0, other arithmetic: 22.1 us -> none  [the longest x1 8.1 us: shards(): jnp.sum(exponent, axis=1)]
  transfers between devices with their start and end apart: 4 -> 3, of which waited for: 4 -> 3; matrix products, arithmetic and copies ran while one was open for 2% -> 0% of each run, Pallas kernels for 0% -> 0%
where the time goes in v2:
time: 102 us; the launch traced here: 101 us
  blocking collectives  52 us (51%)
  Pallas kernels  37.1 us (36%)
  waiting for transfers between devices  6.54 us (6%)
  starting transfers between devices  4.12 us (4%)
    all_to_all x1, blocking collectives, shards(): arrived = lax.all_to_all(paired, ('z_hi', 'dp'), 0, 0, tiled=True)  26.4 us
    all_to_all x1, blocking collectives, shards(): gathered = lax.all_to_all(send, 'dp', 0, 0, tiled=True)  25.7 us
    pallas_call x1, Pallas kernels, class_pass(): pl.pallas_call(class_kernel, in_specs=[pl.BlockSpec(memory_space=pltpu.SM...  25.6 us
    pallas_call x1, Pallas kernels, feed_forward(): pl.pallas_call(ffn_kernel, grid=(rows // block,), in_specs=[pl.BlockSpec(...  8.24 us
    ppermute x1, starting transfers between devices, shards(): other = lax.ppermute(partial, 'z_hi', swap)  4.03 us
    ppermute x1, waiting for transfers between devices, shards(): got = lax.ppermute(give, 'core', swap)  2.74 us
    ppermute x1, waiting for transfers between devices, shards(): other = lax.ppermute(partial, 'z_hi', swap)  2.34 us
  transfers between devices with their start and end apart: 3, of which 3 were waited for; matrix products, arithmetic and copies ran while one was open for 0% of the time, Pallas kernels for 0%

profile of v2, /device:TPU:0, one launch (start us, length us, event | category | flops | bytes accessed | tf_op | source)
XLA Modules:
  0.0 101.4 jit_solution(3848479073272405983)
XLA Ops:
  0.6 0.0 copy-start
  0.6 0.0 copy-start.1
  0.7 8.2 %ffn.1 = f32[16,1024]{1,0:T(8,128)} custom-call(bf16[1024,1024]{1,0:T(8,128)(2,1)} %bitcast.16, f32[1,1024]{1,0:T(1,128)} %bitcast.17, bf16[1024,1024]{1,0:T(8,128)(2,1)} %win_ref.1, bf16[1024,1024]{1,0:T(8,128)(2,1)} %wout_ref.1), custom_call_target="tpu_custom_call" | custom-call | flops 2147483648 | bytes 6291456 | tf_op jit(solution)/shard_map/ffn/pallas_call | solution.py:85
  8.9 0.0 collective-permute-start
  8.9 1.5 %collective-permute-done = f32[16,1024]{1,0:T(8,128)S(1)} collective-permute-done((f32[16,1024]{1,0:T(8,128)}, f32[16,1024]{1,0:T(8,128)S(1)}, u32[]{:S(2)}, u32[]{:S(2)}) %collective-permute-start) | collective-permute-done | bytes 65568 | tf_op jit(solution)/shard_map/ppermute | solution.py:475
  10.4 0.9 add.11.mine_ref
  11.2 4.0 %collective-permute-start.1 = (f32[16,1024]{1,0:T(8,128)S(1)}, f32[16,1024]{1,0:T(8,128)S(1)}, u32[]{:S(2)}, u32[]{:S(2)}) collective-permute-start(f32[16,1024]{1,0:T(8,128)S(1)} %add.11.mine_ref), channel_id=1, source_target_pairs={{0,64},{64,0},{1,65},{65,1},{2,66},{66,2},{3,67},{67,3},{4,68},{68... | collective-permute-start | bytes 196616 | tf_op jit(solution)/shard_map/ppermute | solution.py:476
  15.2 0.1 pad_add_fusion.where_ref
  15.3 2.3 %collective-permute-done.1.other_ref = f32[16,1024]{1,0:T(8,128)S(1)} collective-permute-done((f32[16,1024]{1,0:T(8,128)S(1)}, f32[16,1024]{1,0:T(8,128)S(1)}, u32[]{:S(2)}, u32[]{:S(2)}) %collective-permute-start.1) | collective-permute-done | bytes 65568 | tf_op jit(solution)/shard_map/ppermute | solution.py:476
  17.7 0.0 copy-done
  17.7 0.0 copy-done.1
  17.7 0.9 unit_rows.1
  18.6 25.7 %all_to_all.22 = bf16[32,8,2176]{2,1,0:T(8,128)(2,1)S(1)} all-to-all(bf16[32,8,2176]{2,1,0:T(8,128)(2,1)S(1)} %bitcast.13), channel_id=1, replica_groups=mesh['z_hi'=2,'core'=2,'dp'=32] {'dp'}, dimensions={0} | all-to-all | bytes 2228224 | tf_op jit(solution)/shard_map/all_to_all | solution.py:478
  44.2 25.6 %class_pass.1 = (f32[256,1152]{1,0:T(8,128)S(1)}, bf16[256,1024]{1,0:T(8,128)(2,1)S(1)}, bf16[256,2176]{1,0:T(8,128)(2,1)S(1)}) custom-call(s32[3]{0:T(128)S(1)} %pad_add_fusion.where_ref, bf16[256,2176]{1,0:T(8,128)(2,1)S(1)} %bitcast.14, bf16[8192,1024]{1,0:T(8,128)(2,1)} %centres_ref.1), custom_call_target="tpu_custom_call" | custom-call | flops 17179869184 | bytes 16777216 | tf_op jit(solution)/shard_map/class_pass/pallas_call | solution.py:351
  69.8 0.1 collective-permute-start.2
  69.9 2.7 %collective-permute-done.2.got_ref = bf16[256,2176]{1,0:T(8,128)(2,1)S(1)} collective-permute-done((bf16[256,2176]{1,0:T(8,128)(2,1)S(1)}, bf16[256,2176]{1,0:T(8,128)(2,1)S(1)}, u32[]{:S(2)}, u32[]{:S(2)}) %collective-permute-start.2) | collective-permute-done | bytes 1114144 | tf_op jit(solution)/shard_map/ppermute | solution.py:480
  72.7 0.8 pair_sum.1
  73.4 26.4 %all_to_all.23 = bf16[64,8,1152]{2,1,0:T(8,128)(2,1)S(1)} all-to-all(bf16[64,8,1152]{2,1,0:T(8,128)(2,1)S(1)} %bitcast.12), channel_id=1, replica_groups=mesh['z_hi'=2,'core'=2,'dp'=32] {'z_hi','dp'}, dimensions={0} | all-to-all | bytes 2359296 | tf_op jit(solution)/shard_map/all_to_all | solution.py:482
  99.8 1.6 %home.1 = (f32[1,16]{1,0:T(1,128)}, f32[16,256]{1,0:T(8,128)}) custom-call(s32[3]{0:T(128)S(1)} %pad_add_fusion.where_ref, bf16[512,1152]{1,0:T(8,128)(2,1)S(1)} %bitcast.11, f32[16,1024]{1,0:T(8,128)S(1)} %get-tuple-element.14.unit_ref, f32[16,128]{1,0:T(8,128)S(1)} %get-tuple-element.15.len_ref), custom_call_target="tpu_custom_call" | custom-call | tf_op jit(solution)/shard_map/home/pallas_call | solution.py:443
Async XLA Ops:
  0.6 17.0 %copy-start = (f32[1024]{0:T(1024)S(1)}, f32[1024]{0:T(1024)}, u32[]{:S(2)}) copy-start(f32[1024]{0:T(1024)} %param.11) | copy-start | bytes 12292
  0.6 17.0 %copy-start.1 = (s32[16]{0:T(128)S(1)}, s32[16]{0:T(128)}, u32[]{:S(2)}) copy-start(s32[16]{0:T(128)} %labels_ref.1) | copy-start | bytes 196
  8.9 1.5 %collective-permute-start = (f32[16,1024]{1,0:T(8,128)}, f32[16,1024]{1,0:T(8,128)S(1)}, u32[]{:S(2)}, u32[]{:S(2)}) collective-permute-start(f32[16,1024]{1,0:T(8,128)} %ffn.1), channel_id=1, source_target_pairs={{0,32},{32,0},{1,33},{33,1},{2,34},{34,2},{3,35},{35,3},{4,36},{36... | collective-permute-start | bytes 196616 | tf_op jit(solution)/shard_map/ppermute | solution.py:475
  11.2 6.4 %collective-permute-start.1 = (f32[16,1024]{1,0:T(8,128)S(1)}, f32[16,1024]{1,0:T(8,128)S(1)}, u32[]{:S(2)}, u32[]{:S(2)}) collective-permute-start(f32[16,1024]{1,0:T(8,128)S(1)} %add.11.mine_ref), channel_id=1, source_target_pairs={{0,64},{64,0},{1,65},{65,1},{2,66},{66,2},{3,67},{67,3},{4,68},{68... | collective-permute-start | bytes 196616 | tf_op jit(solution)/shard_map/ppermute | solution.py:476
  69.8 2.8 %collective-permute-start.2 = (bf16[256,2176]{1,0:T(8,128)(2,1)S(1)}, bf16[256,2176]{1,0:T(8,128)(2,1)S(1)}, u32[]{:S(2)}, u32[]{:S(2)}) collective-permute-start(bf16[256,2176]{1,0:T(8,128)(2,1)S(1)} %get-tuple-element.13), channel_id=1, source_target_pairs={{0,32},{32,0},{1,33},{33,1},{2,34},{34,2},{3,35},{35,3},{4,36},{36... | collective-permute-start | bytes 3342344 | tf_op jit(solution)/shard_map/ppermute | solution.py:480

commit v3 on v2

--- a/solution.py
+++ b/solution.py
@@ -48,31 +48,41 @@
     return hi, mid, value - hi - mid
 
 
-def ffn_kernel(tokens_ref, gain_ref, win_ref, wout_ref, out_ref, mean_ref, tok_ref):
+toks = 64
+
+
+def ffn_kernel(tokens_ref, gain_ref, win_ref, wout_hbm, out_ref, mean_ref, tok_ref, wout, sem):
     step = pl.program_id(0)
     block, width = tokens_ref.shape
-    toks = 64
-    per = block // toks
-    wide = tokens_ref[...].astype(f32)
-    normed = layer_norm(wide, gain_ref[...]).astype(bf16)
-    pre = jnp.dot(normed, win_ref[...], preferred_element_type=f32)
-    hidden = (0.5 * pre * (1.0 + lax.erf(pre * math.sqrt(0.5)))).astype(bf16).astype(f32)
-    for k in range(per):
-        mean_ref[pl.ds(step * per + k, 1), :] = (
-            jnp.sum(hidden[k * toks : (k + 1) * toks], axis=0, keepdims=True) * (1.0 / toks)
-        )
-        tok_ref[pl.ds(step * per + k, 1), :] = (
-            jnp.sum(wide[k * toks : (k + 1) * toks], axis=0, keepdims=True) * (0.25 / toks)
-        )
+    sub = 256
+    per = sub // toks
+    fetch = pltpu.make_async_copy(wout_hbm, wout, sem)
+
+    @pl.when(step == 0)
+    def _():
+        fetch.start()
+
+    image = lax.broadcasted_iota(jnp.int32, (8, sub), 0)
+    member = (lax.broadcasted_iota(jnp.int32, (8, sub), 1) // toks == image).astype(f32).astype(bf16)
+    for k in range(block // sub):
+        rows = tokens_ref[k * sub : (k + 1) * sub, :]
+        normed = layer_norm(rows.astype(f32), gain_ref[...]).astype(bf16)
+        pre = jnp.dot(normed, win_ref[...], preferred_element_type=f32)
+        hidden = (0.5 * pre * (1.0 + lax.erf(pre * math.sqrt(0.5)))).astype(bf16)
+        mean = jnp.dot(member, hidden, preferred_element_type=f32) * (1.0 / toks)
+        tok = jnp.dot(member, rows, preferred_element_type=f32) * (0.25 / toks)
+        for q in range(per):
+            at = pl.ds(step * (block // toks) + k * per + q, 1)
+            mean_ref[at, :] = mean[q : q + 1]
+            tok_ref[at, :] = tok[q : q + 1]
 
     @pl.when(step == pl.num_programs(0) - 1)
     def _():
+        fetch.wait()
         mean = mean_ref[...]
         hi = mean.astype(bf16)
         lo = (mean - hi.astype(f32)).astype(bf16)
-        both = jnp.dot(
-            jnp.concatenate([hi, lo], axis=0), wout_ref[...], preferred_element_type=f32
-        )
+        both = jnp.dot(jnp.concatenate([hi, lo], axis=0), wout[...], preferred_element_type=f32)
         images = mean.shape[0]
         out_ref[...] = both[:images] + both[images:] + tok_ref[...]
 
@@ -80,8 +90,8 @@
 def feed_forward(tokens, gain, weight_in, weight_out):
     rows, width = tokens.shape
     hidden = weight_in.shape[1]
-    images = rows // 64
-    block = 256
+    images = rows // toks
+    block = 512
     return pl.pallas_call(
         ffn_kernel,
         grid=(rows // block,),
@@ -89,12 +99,17 @@
             pl.BlockSpec((block, width), lambda i: (i, 0)),
             pl.BlockSpec((1, width), lambda i: (0, 0)),
             pl.BlockSpec((width, hidden), lambda i: (0, 0)),
-            pl.BlockSpec((hidden, width), lambda i: (0, 0)),
+            pl.BlockSpec(memory_space=pltpu.HBM),
         ],
         out_specs=pl.BlockSpec((images, width), lambda i: (0, 0)),
-        out_shape=jax.ShapeDtypeStruct((images, width), f32),
-        scratch_shapes=[pltpu.VMEM((images, hidden), f32), pltpu.VMEM((images, width), f32)],
-        compiler_params=params(56),
+        out_shape=pltpu.VMEM((images, width), f32),
+        scratch_shapes=[
+            pltpu.VMEM((images, hidden), f32),
+            pltpu.VMEM((images, width), f32),
+            pltpu.VMEM((hidden, width), bf16),
+            pltpu.SemaphoreType.DMA,
+        ],
+        compiler_params=params(58),
         cost_estimate=pl.CostEstimate(
             flops=2 * rows * width * hidden, bytes_accessed=6 << 20, transcendentals=rows * hidden
         ),
@@ -140,7 +155,7 @@
             pl.BlockSpec(memory_space=pltpu.VMEM),
         ],
         out_shape=(
-            jax.ShapeDtypeStruct((homes * images // 2, 2 * width + lanes), bf16),
+            pltpu.VMEM((homes * images // 2, 2 * width + lanes), bf16),
             jax.ShapeDtypeStruct((images, width), f32),
             jax.ShapeDtypeStruct((images, lanes), f32),
         ),
@@ -189,7 +204,7 @@
         at = pl.ds(pl.multiple_of(i * block, block), block)
         return pltpu.make_async_copy(centres_ref.at[at, :], held.at[at, :], sems.at[i])
 
-    for i in range(pieces):
+    for i in range(2):
         fetch(i).start()
 
     coded = all_ref[:, 2 * width :]
@@ -245,6 +260,11 @@
     def step(t, c):
         base = pl.multiple_of(t * block, block)
         fetch(t).wait()
+
+        @pl.when(t + 2 < pieces)
+        def _():
+            fetch(t + 2).start()
+
         centres = held[pl.ds(base, block), :]
         cosine = lax.dot_general(unit[...], centres, turned, preferred_element_type=f32)
         lane = lax.broadcasted_iota(jnp.int32, (images, lanes), 1) + base
@@ -403,7 +423,7 @@
     rows, width = keep_rows.shape
     return pl.pallas_call(
         pair_kernel,
-        out_shape=jax.ShapeDtypeStruct((2 * rows, width + lanes), bf16),
+        out_shape=pltpu.VMEM((2 * rows, width + lanes), bf16),
         compiler_params=params(12),
         name="pair_sum",
     )(keep, keep_rows, got)

time: 102 us -> 99.7 us (0.977)
  Pallas kernels: 37.1 us -> 35.6 us
    pallas_call x1, Pallas kernels: 8.24 us -> 6.78 us  [feed_forward(): pl.pallas_call(ffn_kernel, grid=(rows // block,), in_specs=[pl.BlockSpec(...]
where the time goes in v3:
time: 99.7 us; the launch traced here: 99.8 us
  blocking collectives  52.9 us (53%)
  Pallas kernels  35.6 us (36%)
  waiting for transfers between devices  6.31 us (6%)
  starting transfers between devices  4.21 us (4%)
    all_to_all x1, blocking collectives, shards(): arrived = lax.all_to_all(paired, ('z_hi', 'dp'), 0, 0, tiled=True)  27.3 us
    all_to_all x1, blocking collectives, shards(): gathered = lax.all_to_all(send, 'dp', 0, 0, tiled=True)  25.7 us
    pallas_call x1, Pallas kernels, class_pass(): pl.pallas_call(class_kernel, in_specs=[pl.BlockSpec(memory_space=pltpu.SM...  25.6 us
    pallas_call x1, Pallas kernels, feed_forward(): pl.pallas_call(ffn_kernel, grid=(rows // block,), in_specs=[pl.BlockSpec(...  6.78 us
    ppermute x1, starting transfers between devices, shards(): other = lax.ppermute(partial, 'z_hi', swap)  4.04 us
    ppermute x1, waiting for transfers between devices, shards(): got = lax.ppermute(give, 'core', swap)  2.74 us
    ppermute x1, waiting for transfers between devices, shards(): other = lax.ppermute(partial, 'z_hi', swap)  2.34 us
  transfers between devices with their start and end apart: 3, of which 3 were waited for; matrix products, arithmetic and copies ran while one was open for 0% of the time, Pallas kernels for 0%

profile of v3, /device:TPU:0, one launch (start us, length us, event | category | flops | bytes accessed | tf_op | source)
XLA Modules:
  0.0 99.8 jit_solution(15861978771627210955)
XLA Ops:
  0.6 0.0 copy-start
  0.6 0.0 copy-start.1
  0.7 6.8 %ffn.1 = f32[16,1024]{1,0:T(8,128)S(1)} custom-call(bf16[1024,1024]{1,0:T(8,128)(2,1)} %bitcast.16, f32[1,1024]{1,0:T(1,128)} %bitcast.17, bf16[1024,1024]{1,0:T(8,128)(2,1)} %win_ref.1, bf16[1024,1024]{1,0:T(8,128)(2,1)} %wout_hbm.1), custom_call_target="tpu_custom_call" | custom-call | flops 2147483648 | bytes 6291456 | tf_op jit(solution)/shard_map/ffn/pallas_call | solution.py:95
  7.4 0.1 collective-permute-start
  7.5 1.2 %collective-permute-done = f32[16,1024]{1,0:T(8,128)S(1)} collective-permute-done((f32[16,1024]{1,0:T(8,128)S(1)}, f32[16,1024]{1,0:T(8,128)S(1)}, u32[]{:S(2)}, u32[]{:S(2)}) %collective-permute-start) | collective-permute-done | bytes 65568 | tf_op jit(solution)/shard_map/ppermute | solution.py:495
  8.8 4.0 %collective-permute-start.1 = (f32[16,1024]{1,0:T(8,128)S(1)}, f32[16,1024]{1,0:T(8,128)S(1)}, u32[]{:S(2)}, u32[]{:S(2)}) collective-permute-start(f32[16,1024]{1,0:T(8,128)S(1)} %add.11.mine_ref), channel_id=1, source_target_pairs={{0,64},{64,0},{1,65},{65,1},{2,66},{66,2},{3,67},{67,3},{4,68},{68... | collective-permute-start | bytes 196616 | tf_op jit(solution)/shard_map/ppermute | solution.py:496
  12.8 0.1 pad_add_fusion.where_ref
  12.9 2.3 %collective-permute-done.1.other_ref = f32[16,1024]{1,0:T(8,128)S(1)} collective-permute-done((f32[16,1024]{1,0:T(8,128)S(1)}, f32[16,1024]{1,0:T(8,128)S(1)}, u32[]{:S(2)}, u32[]{:S(2)}) %collective-permute-start.1) | collective-permute-done | bytes 65568 | tf_op jit(solution)/shard_map/ppermute | solution.py:496
  15.2 0.0 copy-done
  15.2 0.0 copy-done.1
  15.2 0.9 unit_rows.1
  16.1 25.7 %all_to_all.22 = bf16[32,8,2176]{2,1,0:T(8,128)(2,1)S(1)} all-to-all(bf16[32,8,2176]{2,1,0:T(8,128)(2,1)S(1)} %bitcast.13), channel_id=1, replica_groups=mesh['z_hi'=2,'core'=2,'dp'=32] {'dp'}, dimensions={0} | all-to-all | bytes 2228224 | tf_op jit(solution)/shard_map/all_to_all | solution.py:498
  41.8 25.6 %class_pass.1 = (f32[256,1152]{1,0:T(8,128)S(1)}, bf16[256,1024]{1,0:T(8,128)(2,1)S(1)}, bf16[256,2176]{1,0:T(8,128)(2,1)S(1)}) custom-call(s32[3]{0:T(128)S(1)} %pad_add_fusion.where_ref, bf16[256,2176]{1,0:T(8,128)(2,1)S(1)} %bitcast.14, bf16[8192,1024]{1,0:T(8,128)(2,1)} %centres_ref.1), custom_call_target="tpu_custom_call" | custom-call | flops 17179869184 | bytes 16777216 | tf_op jit(solution)/shard_map/class_pass/pallas_call | solution.py:371
  67.4 0.1 collective-permute-start.2
  67.5 2.7 %collective-permute-done.2.got_ref = bf16[256,2176]{1,0:T(8,128)(2,1)S(1)} collective-permute-done((bf16[256,2176]{1,0:T(8,128)(2,1)S(1)}, bf16[256,2176]{1,0:T(8,128)(2,1)S(1)}, u32[]{:S(2)}, u32[]{:S(2)}) %collective-permute-start.2) | collective-permute-done | bytes 1114144 | tf_op jit(solution)/shard_map/ppermute | solution.py:500
  70.2 0.8 pair_sum.1
  71.0 27.3 %all_to_all.23 = bf16[64,8,1152]{2,1,0:T(8,128)(2,1)S(1)} all-to-all(bf16[64,8,1152]{2,1,0:T(8,128)(2,1)S(1)} %bitcast.12), channel_id=1, replica_groups=mesh['z_hi'=2,'core'=2,'dp'=32] {'z_hi','dp'}, dimensions={0} | all-to-all | bytes 2359296 | tf_op jit(solution)/shard_map/all_to_all | solution.py:502
  98.3 1.6 %home.1 = (f32[1,16]{1,0:T(1,128)}, f32[16,256]{1,0:T(8,128)}) custom-call(s32[3]{0:T(128)S(1)} %pad_add_fusion.where_ref, bf16[512,1152]{1,0:T(8,128)(2,1)S(1)} %bitcast.11, f32[16,1024]{1,0:T(8,128)S(1)} %get-tuple-element.14.unit_ref, f32[16,128]{1,0:T(8,128)S(1)} %get-tuple-element.15.len_ref), custom_call_target="tpu_custom_call" | custom-call | tf_op jit(solution)/shard_map/home/pallas_call | solution.py:463
  (1 shorter events, 0.0 us)
Async XLA Ops:
  0.6 14.6 %copy-start = (f32[1024]{0:T(1024)S(1)}, f32[1024]{0:T(1024)}, u32[]{:S(2)}) copy-start(f32[1024]{0:T(1024)} %param.11) | copy-start | bytes 12292
  0.6 14.6 %copy-start.1 = (s32[16]{0:T(128)S(1)}, s32[16]{0:T(128)}, u32[]{:S(2)}) copy-start(s32[16]{0:T(128)} %labels_ref.1) | copy-start | bytes 196
  7.4 1.3 %collective-permute-start = (f32[16,1024]{1,0:T(8,128)S(1)}, f32[16,1024]{1,0:T(8,128)S(1)}, u32[]{:S(2)}, u32[]{:S(2)}) collective-permute-start(f32[16,1024]{1,0:T(8,128)S(1)} %ffn.1), channel_id=1, source_target_pairs={{0,32},{32,0},{1,33},{33,1},{2,34},{34,2},{3,35},{35,3},{4,36},{36... | collective-permute-start | bytes 196616 | tf_op jit(solution)/shard_map/ppermute | solution.py:495
  8.8 6.5 %collective-permute-start.1 = (f32[16,1024]{1,0:T(8,128)S(1)}, f32[16,1024]{1,0:T(8,128)S(1)}, u32[]{:S(2)}, u32[]{:S(2)}) collective-permute-start(f32[16,1024]{1,0:T(8,128)S(1)} %add.11.mine_ref), channel_id=1, source_target_pairs={{0,64},{64,0},{1,65},{65,1},{2,66},{66,2},{3,67},{67,3},{4,68},{68... | collective-permute-start | bytes 196616 | tf_op jit(solution)/shard_map/ppermute | solution.py:496
  67.4 2.8 %collective-permute-start.2 = (bf16[256,2176]{1,0:T(8,128)(2,1)S(1)}, bf16[256,2176]{1,0:T(8,128)(2,1)S(1)}, u32[]{:S(2)}, u32[]{:S(2)}) collective-permute-start(bf16[256,2176]{1,0:T(8,128)(2,1)S(1)} %get-tuple-element.13), channel_id=1, source_target_pairs={{0,32},{32,0},{1,33},{33,1},{2,34},{34,2},{3,35},{35,3},{4,36},{36... | collective-permute-start | bytes 3342344 | tf_op jit(solution)/shard_map/ppermute | solution.py:500

commit v4 on v3

--- a/solution.py
+++ b/solution.py
@@ -1,3 +1,4 @@
+import functools
 import math
 
 import jax
@@ -13,6 +14,8 @@
 lanes = 128
 digits = 3
 pieces = 8
+columns = 256
+batch = 4
 f32 = jnp.float32
 bf16 = jnp.bfloat16
 
@@ -124,18 +127,21 @@
     length = jnp.sqrt(jnp.sum(embedding * embedding, axis=1, keepdims=True) + 1e-06)
     unit = (embedding / length).astype(bf16).astype(f32)
     half = images // 2
+    first = where_ref[1] == 1
     row = lax.broadcasted_iota(jnp.int32, (half, lanes), 0)
     lane = lax.broadcasted_iota(jnp.int32, (half, lanes), 1)
     label = jnp.zeros((half, lanes), jnp.int32)
-    for h in range(2):
-        for r in range(half):
-            here = jnp.logical_and(row == r, lane // digits == h)
-            label = jnp.where(here, labels_ref[h * half + r], label)
-    place = lane % digits
+    for r in range(half):
+        label = jnp.where(
+            row == r, jnp.where(first, labels_ref[r], labels_ref[half + r]), label
+        )
     coded = jnp.where(
-        place == 0, label & 127, jnp.where(place == 1, (label >> 7) & 127, label >> 14)
-    )
-    payload = jnp.concatenate([unit[:half], unit[half:], coded.astype(f32)], axis=1)
+        lane == 0,
+        label & 127,
+        jnp.where(lane == 1, (label >> 7) & 127, jnp.where(lane == 2, label >> 14, 0)),
+    )
+    chosen = jnp.where(first, unit[:half], unit[half:])
+    payload = jnp.concatenate([chosen, coded.astype(f32)], axis=1)
     payload = jnp.concatenate([payload, payload], axis=0).astype(bf16)
     for d in range(send_ref.shape[0] // images):
         send_ref[d * images : (d + 1) * images, :] = payload
@@ -155,7 +161,7 @@
             pl.BlockSpec(memory_space=pltpu.VMEM),
         ],
         out_shape=(
-            pltpu.VMEM((homes * images // 2, 2 * width + lanes), bf16),
+            pltpu.VMEM((homes * images // 2, width + lanes), bf16),
             jax.ShapeDtypeStruct((images, width), f32),
             jax.ShapeDtypeStruct((images, lanes), f32),
         ),
@@ -164,8 +170,8 @@
     )(where, labels, mine, other, gain)
 
 
-def digit_weights(shape, axis, h):
-    at = lax.broadcasted_iota(jnp.int32, shape, axis) - h * digits
+def digit_weights(shape, axis):
+    at = lax.broadcasted_iota(jnp.int32, shape, axis)
     return jnp.where(
         at == 0, 1.0, jnp.where(at == 1, 128.0, jnp.where(at == 2, 16384.0, 0.0))
     ).astype(bf16)
@@ -174,65 +180,46 @@
 group_size = 16
 
 
-def class_kernel(
-    where_ref,
-    all_ref,
-    centres_ref,
-    keep_ref,
-    keep_row_ref,
-    send_ref,
-    held,
-    unit,
-    acc,
-    tot,
-    cos_row,
-    lab,
-    lab_s,
-    found_s,
-    lab_sem,
-    sems,
-):
+def class_kernel(second, where_ref, all_ref, centres_ref, *refs):
+    if second:
+        inverse_ref, keep_ref, keep_row_ref, send_ref, *refs = refs
+    else:
+        keep_ref, keep_row_ref, send_ref, inverse_ref, *refs = refs
+    held, acc, tot, cos_row, lab, lab_s, found_s, lab_sem, sems = refs
     offset, core = where_ref[0], where_ref[1]
-    rows = all_ref.shape[0]
-    images = 2 * rows
+    images = all_ref.shape[0]
     count, width = centres_ref.shape
-    block = count // pieces
+    piece = count // pieces
     half, part = width // 2, width // 4
     groups = images // group_size
 
     def fetch(i):
-        at = pl.ds(pl.multiple_of(i * block, block), block)
+        at = pl.ds(pl.multiple_of(i * piece, piece), piece)
         return pltpu.make_async_copy(centres_ref.at[at, :], held.at[at, :], sems.at[i])
 
-    for i in range(2):
+    for i in range(3):
         fetch(i).start()
 
-    coded = all_ref[:, 2 * width :]
+    coded = all_ref[:, width:]
     turned = (((1,), (1,)), ((), ()))
-    for h in range(2):
-        unit[h * rows : (h + 1) * rows, :] = all_ref[:, h * width : (h + 1) * width]
-        lab[:, h * rows : (h + 1) * rows] = lax.dot_general(
-            digit_weights((8, lanes), 1, h), coded, turned, preferred_element_type=f32
-        ).astype(jnp.int32) - offset
-    row = lab[:, :images]
+    row = lax.dot_general(
+        digit_weights((8, lanes), 1), coded, turned, preferred_element_type=f32
+    ).astype(jnp.int32) - offset
     member = lax.broadcasted_iota(jnp.int32, (images, lanes), 0) // group_size
     member = (member == lax.broadcasted_iota(jnp.int32, (images, lanes), 1)).astype(bf16)
     inside = jnp.logical_and(row >= 0, row < count).astype(f32).astype(bf16)
+    lab[:, :images] = row
     lab[:, images:] = jnp.dot(inside, member, preferred_element_type=f32).astype(jnp.int32)
     copy = pltpu.make_async_copy(lab, lab_s, lab_sem)
     copy.start()
-    local = jnp.concatenate(
-        [
-            jnp.dot(coded, digit_weights((lanes, lanes), 0, h), preferred_element_type=f32)
-            for h in range(2)
-        ],
-        axis=0,
+    local = (
+        jnp.dot(coded, digit_weights((lanes, lanes), 0), preferred_element_type=f32)
     ).astype(jnp.int32) - offset
     acc[...] = jnp.zeros(acc.shape, f32)
     tot[...] = jnp.zeros(tot.shape, f32)
     cos_row[...] = jnp.zeros(cos_row.shape, f32)
     keep_row_ref[...] = jnp.zeros(keep_row_ref.shape, bf16)
-    send_ref[:, width : 2 * width] = jnp.zeros((rows, width), bf16)
+    send_ref[:, half:width] = jnp.zeros((images, half), bf16)
     copy.wait()
     found_s[images] = 0
 
@@ -257,84 +244,93 @@
         jnp.int32, (lanes, lanes), 1
     )
 
-    def step(t, c):
-        base = pl.multiple_of(t * block, block)
-        fetch(t).wait()
-
-        @pl.when(t + 2 < pieces)
-        def _():
-            fetch(t + 2).start()
+    def step(first, joined, ahead):
+        base = pl.multiple_of(first * piece, piece)
+        block = joined * piece
+        for q in range(joined):
+            fetch(first + q).wait()
+        for q in ahead:
+            fetch(first + q).start()
 
         centres = held[pl.ds(base, block), :]
-        cosine = lax.dot_general(unit[...], centres, turned, preferred_element_type=f32)
+        cosine = lax.dot_general(
+            all_ref[:, :width], centres, turned, preferred_element_type=f32
+        )
         lane = lax.broadcasted_iota(jnp.int32, (images, lanes), 1) + base
         parts = []
         total = tot[...]
         for j in range(block // lanes):
-            wide = held[pl.ds(base + j * lanes, lanes), :].astype(f32)
-            square = jnp.sum(wide * wide, axis=1, keepdims=True)
-            square = jnp.sum(jnp.where(diagonal, square, 0.0), axis=0, keepdims=True)
-            inverse = lax.rsqrt(square + 1e-06)
+            at = pl.ds(base + j * lanes, lanes)
+            if second:
+                inverse = inverse_ref[:, at]
+            else:
+                wide = held[at, :].astype(f32)
+                square = jnp.sum(wide * wide, axis=1, keepdims=True)
+                square = jnp.sum(jnp.where(diagonal, square, 0.0), axis=0, keepdims=True)
+                inverse = lax.rsqrt(square + 1e-06)
+                inverse_ref[:, at] = inverse
             value = jnp.exp2(cosine[:, j * lanes : (j + 1) * lanes] * (inverse * exp2_scale))
             value = jnp.where(local == lane + j * lanes, 0.0, value)
             total = total + value
             parts.append((value * inverse).astype(bf16))
         tot[...] = total
-        acc[...] += jnp.dot(jnp.concatenate(parts, axis=1), centres, preferred_element_type=f32)
+        weight = jnp.concatenate(parts, axis=1)
+        for n in range(0, width, columns):
+            cols = slice(n, n + columns)
+            acc[:, cols] += jnp.dot(weight, centres[:, cols], preferred_element_type=f32)
+
+    def pair(t, c):
+        step(1 + 2 * t, 2, (4, 5))
         return c
 
-    lax.fori_loop(0, pieces, step, 0)
+    step(0, 1, (3, 4))
+    lax.fori_loop(0, (pieces - 6) // 2, pair, 0)
+    step(pieces - 5, 2, (4,))
+    step(pieces - 3, 2, ())
+    step(pieces - 1, 1, ())
 
     sub = lax.broadcasted_iota(jnp.int32, (16, width), 0)
 
     def take(k, c):
-        i = found_s[k]
-        at = lab_s[0, i]
-        raw = held[pl.ds(pl.multiple_of((at >> 4) << 4, 16), 16), :].astype(f32)
-        raw = jnp.sum(jnp.where(sub == (at & 15), raw, 0.0), axis=0, keepdims=True)
-        found = raw * lax.rsqrt(jnp.sum(raw * raw, axis=1, keepdims=True) + 1e-06)
-        found = found.astype(bf16).astype(f32)
-        mine = sub == (i & 15)
-        first = pl.multiple_of((i >> 4) << 4, 16)
-        image = unit[pl.ds(first, 16), :].astype(f32)
-        cos = jnp.sum(jnp.where(mine, image * found, 0.0), axis=1, keepdims=True)
-        cos_row[pl.ds(first, 16), :] = jnp.where(
-            mine[:, :lanes], cos, cos_row[pl.ds(first, 16), :]
-        )
-        even = jnp.concatenate([found[:, :part], found[:, half : half + part]], axis=1)
-        odd = jnp.concatenate([found[:, part:half], found[:, half + part :]], axis=1)
-        kept = jnp.where(core == 0, even, odd)
-        sent = jnp.where(core == 0, odd, even)
-        for h in range(2):
-
-            @pl.when((i >= rows) == (h == 1))
-            def _():
-                here = pl.ds(pl.multiple_of(first - h * rows, 16), 16)
-                for ref, start, value in ((keep_row_ref, 0, kept), (send_ref, width, sent)):
-                    cols = slice(start + h * half, start + (h + 1) * half)
-                    ref[here, cols] = jnp.where(
-                        mine[:, :half], value, ref[here, cols].astype(f32)
-                    ).astype(bf16)
-
+        ready = []
+        for q in range(batch):
+            i = found_s[jnp.minimum(k * batch + q, found_s[images] - 1)]
+            at = lab_s[0, i]
+            raw = held[pl.ds(pl.multiple_of((at >> 4) << 4, 16), 16), :].astype(f32)
+            raw = jnp.sum(jnp.where(sub == (at & 15), raw, 0.0), axis=0, keepdims=True)
+            found = raw * lax.rsqrt(jnp.sum(raw * raw, axis=1, keepdims=True) + 1e-06)
+            found = found.astype(bf16).astype(f32)
+            mine = sub == (i & 15)
+            here = pl.ds(pl.multiple_of((i >> 4) << 4, 16), 16)
+            image = all_ref[here, :width].astype(f32)
+            cos = jnp.sum(jnp.where(mine, image * found, 0.0), axis=1, keepdims=True)
+            even = jnp.concatenate([found[:, :part], found[:, half : half + part]], axis=1)
+            odd = jnp.concatenate([found[:, part:half], found[:, half + part :]], axis=1)
+            kept = jnp.where(core == 0, even, odd)
+            sent = jnp.where(core == 0, odd, even)
+            ready.append((mine, here, cos, kept, sent))
+        for mine, here, cos, kept, sent in ready:
+            cos_row[here, :] = jnp.where(mine[:, :lanes], cos, cos_row[here, :])
+            for ref, start, value in ((keep_row_ref, 0, kept), (send_ref, half, sent)):
+                cols = slice(start, start + half)
+                ref[here, cols] = jnp.where(
+                    mine[:, :half], value, ref[here, cols].astype(f32)
+                ).astype(bf16)
         return c
 
-    lax.fori_loop(0, found_s[images], take, 0)
-
-    extras = []
-    for h in range(2):
-        at = slice(h * rows, (h + 1) * rows)
-        for group in range(2):
-            cols = slice(h * half + group * part, h * half + (group + 1) * part)
-            keep_at = pl.multiple_of((2 * group + core) * part, part)
-            send_at = pl.multiple_of((2 * group + 1 - core) * part, part)
-            keep_ref[:, cols] = acc[at, pl.ds(keep_at, part)]
-            send_ref[:, cols] = acc[at, pl.ds(send_at, part)].astype(bf16)
-        total = jnp.sum(tot[at, :], axis=1, keepdims=True)
-        inner = jnp.sum(acc[at, :] * unit[at, :].astype(f32), axis=1, keepdims=True)
-        extras.append((total, inner, cos_row[at, :1]))
-    extra = pack_extra(extras)
-    keep_ref[:, width:] = extra
-    send_ref[:, 2 * width :] = extra.astype(bf16)
+    lax.fori_loop(0, (found_s[images] + batch - 1) // batch, take, 0)
+
+    for group in range(2):
+        cols = slice(group * part, (group + 1) * part)
+        keep_at = pl.multiple_of((2 * group + core) * part, part)
+        send_at = pl.multiple_of((2 * group + 1 - core) * part, part)
+        keep_ref[:, cols] = acc[:, pl.ds(keep_at, part)]
+        send_ref[:, cols] = acc[:, pl.ds(send_at, part)].astype(bf16)
+    total = jnp.sum(tot[...], axis=1, keepdims=True)
+    inner = jnp.sum(acc[...] * all_ref[:, :width].astype(f32), axis=1, keepdims=True)
+    extra = pack_extra([(total, inner, cos_row[:, :1])])
+    keep_ref[:, half:] = extra
+    send_ref[:, width:] = extra.astype(bf16)
 
 
 def pack_extra(halves):
@@ -350,9 +346,9 @@
     return out
 
 
-def unpack_extra(extra):
+def unpack_extra(extra, halves_held):
     halves = []
-    for h in range(2):
+    for h in range(halves_held):
         values = []
         for k in range(3 * h, 3 * h + 3):
             values.append(
@@ -364,25 +360,28 @@
     return halves
 
 
-def class_pass(where, gathered, centres):
-    rows = gathered.shape[0]
-    images = 2 * rows
+def class_pass(where, gathered, centres, inverse=None):
+    images = gathered.shape[0]
     count, width = centres.shape
+    half = width // 2
+    second = inverse is not None
+    vmem = pl.BlockSpec(memory_space=pltpu.VMEM)
+    outs = (
+        jax.ShapeDtypeStruct((images, half + lanes), f32),
+        jax.ShapeDtypeStruct((images, half), bf16),
+        jax.ShapeDtypeStruct((images, width + lanes), bf16),
+    )
     return pl.pallas_call(
-        class_kernel,
+        functools.partial(class_kernel, second),
         in_specs=[
             pl.BlockSpec(memory_space=pltpu.SMEM),
-            pl.BlockSpec(memory_space=pltpu.VMEM),
+            vmem,
             pl.BlockSpec(memory_space=pltpu.HBM),
-        ],
-        out_shape=(
-            jax.ShapeDtypeStruct((rows, width + lanes), f32),
-            jax.ShapeDtypeStruct((rows, width), bf16),
-            jax.ShapeDtypeStruct((rows, 2 * width + lanes), bf16),
-        ),
+        ]
+        + [vmem] * second,
+        out_shape=outs if second else (*outs, jax.ShapeDtypeStruct((1, count), f32)),
         scratch_shapes=[
             pltpu.VMEM((count, width), bf16),
-            pltpu.VMEM((images, width), bf16),
             pltpu.VMEM((images, width), f32),
             pltpu.VMEM((images, lanes), f32),
             pltpu.VMEM((images, lanes), f32),
@@ -399,34 +398,47 @@
             transcendentals=images * count,
         ),
         name="class_pass",
-    )(where, gathered, centres)
-
-
-def pair_kernel(keep_ref, keep_row_ref, got_ref, out_ref):
-    rows, width = keep_row_ref.shape
-    half, part = width // 2, width // 4
-    summed = keep_ref[...] + jnp.concatenate(
-        [got_ref[:, :width].astype(f32), got_ref[:, 2 * width :].astype(f32)], axis=1
-    )
-    target = keep_row_ref[...] + got_ref[:, width : 2 * width]
-    extra = pack_extra(unpack_extra(summed[:, width:])).astype(bf16)
+    )(where, gathered, centres, *([inverse] if second else []))
+
+
+def pair_kernel(where_ref, *refs):
+    out_ref = refs[-1]
+    rows, half = refs[1].shape
+    width, part = 2 * half, half // 2
+    sums, targets, extras = [], [], []
+    for keep_ref, keep_row_ref, got_ref in (refs[0:3], refs[3:6]):
+        sums.append((keep_ref[:, :half] + got_ref[:, :half].astype(f32)).astype(bf16))
+        targets.append(keep_row_ref[...] + got_ref[:, half:width])
+        extras.append(keep_ref[:, half:] + got_ref[:, width:].astype(f32))
+    swapped = where_ref[1] == 0
+    extra = pack_extra(
+        [
+            unpack_extra(jnp.where(swapped, extras[1 - h], extras[h]), 1)[0]
+            for h in range(2)
+        ]
+    ).astype(bf16)
+    for h in range(2):
+        summed = jnp.where(swapped, sums[1 - h], sums[h])
+        target = jnp.where(swapped, targets[1 - h], targets[h])
+        for group in range(2):
+            at = slice(group * rows, (group + 1) * rows)
+            cols = slice(group * part, (group + 1) * part)
+            out_ref[at, h * part : (h + 1) * part] = summed[:, cols]
+            out_ref[at, half + h * part : half + (h + 1) * part] = target[:, cols]
     for group in range(2):
-        at = slice(group * rows, (group + 1) * rows)
-        for h in range(2):
-            cols = slice(h * half + group * part, h * half + (group + 1) * part)
-            out_ref[at, h * part : (h + 1) * part] = summed[:, cols].astype(bf16)
-            out_ref[at, half + h * part : half + (h + 1) * part] = target[:, cols]
-        out_ref[at, width:] = extra
-
-
-def pair_sum(keep, keep_rows, got):
-    rows, width = keep_rows.shape
+        out_ref[group * rows : (group + 1) * rows, width:] = extra
+
+
+def pair_sum(where, *arrays):
+    rows, half = arrays[1].shape
     return pl.pallas_call(
         pair_kernel,
-        out_shape=pltpu.VMEM((2 * rows, width + lanes), bf16),
+        in_specs=[pl.BlockSpec(memory_space=pltpu.SMEM)]
+        + [pl.BlockSpec(memory_space=pltpu.VMEM)] * len(arrays),
+        out_shape=pltpu.VMEM((2 * rows, 2 * half + lanes), bf16),
         compiler_params=params(12),
         name="pair_sum",
-    )(keep, keep_rows, got)
+    )(where, *arrays)
 
 
 def home_kernel(where_ref, got_ref, unit_ref, len_ref, loss_ref, grad_ref):
@@ -440,7 +452,7 @@
     row = lax.broadcasted_iota(jnp.int32, (half, images), 0)
     lane = lax.broadcasted_iota(jnp.int32, (half, images), 1)
     loss_row = jnp.zeros((1, images), f32)
-    for h, (rest, inner, cos) in enumerate(unpack_extra(summed[:, 4 * part :])):
+    for h, (rest, inner, cos) in enumerate(unpack_extra(summed[:, 4 * part :], 2)):
         at = slice(h * half, (h + 1) * half)
         gradient = summed[:, h * part : (h + 1) * part]
         target = summed[:, (2 + h) * part : (3 + h) * part]
@@ -496,9 +508,12 @@
     other = lax.ppermute(partial, "z_hi", swap)
     send, unit, length = unit_rows_of(where, labels, partial, other, final_gain[None], homes)
     gathered = lax.all_to_all(send, "dp", 0, 0, tiled=True)
-    keep, keep_rows, give = class_pass(where, gathered, centres)
+    crossed = lax.ppermute(gathered, "core", swap)
+    keep, keep_rows, give, inverse = class_pass(where, gathered, centres)
     got = lax.ppermute(give, "core", swap)
-    paired = pair_sum(keep, keep_rows, got)
+    keep_2, keep_rows_2, give_2 = class_pass(where, crossed, centres, inverse)
+    got_2 = lax.ppermute(give_2, "core", swap)
+    paired = pair_sum(where, keep, keep_rows, got_2, keep_2, keep_rows_2, got)
     arrived = lax.all_to_all(paired, ("z_hi", "dp"), 0, 0, tiled=True)
     loss, grad = home(where, arrived, unit, length)
     return (loss[0], grad)

time: 99.7 us -> 95.6 us (0.959)
  blocking collectives: 52.9 us -> 46.6 us
  Pallas kernels: 35.6 us -> 37.8 us
    all_to_all x1, blocking collectives: 25.7 us -> 20 us  [shards(): gathered = lax.all_to_all(send, 'dp', 0, 0, tiled=True)]
    ppermute x1, waiting for transfers between devices: 2.74 us -> 0.01 us  [shards(): got = lax.ppermute(give, 'core', swap)]
    pallas_call x2 -> x3, Pallas kernels: 26.3 us -> 28.6 us  [the longest x2 27.2 us: class_pass(): pl.pallas_call(functools.partial(class_kernel, second), in_specs=[pl.Bloc...]
    ppermute x0 -> x2, waiting for transfers between devices: none -> 1.98 us  [the longest x1 1.98 us: shards(): got_2 = lax.ppermute(give_2, 'core', swap)]
  transfers between devices with their start and end apart: 3 -> 5, of which waited for: 3 -> 3; matrix products, arithmetic and copies ran while one was open for 0% -> 0% of each run, Pallas kernels for 0% -> 28%
where the time goes in v4:
time: 95.6 us; the launch traced here: 95.5 us
  blocking collectives  46.6 us (49%)
  Pallas kernels  37.8 us (40%)
  waiting for transfers between devices  5.55 us (6%)
  starting transfers between devices  4.75 us (5%)
    pallas_call x2, Pallas kernels, class_pass(): pl.pallas_call(functools.partial(class_kernel, second), in_specs=[pl.Bloc...  27.2 us
    all_to_all x1, blocking collectives, shards(): arrived = lax.all_to_all(paired, ('z_hi', 'dp'), 0, 0, tiled=True)  26.6 us
    all_to_all x1, blocking collectives, shards(): gathered = lax.all_to_all(send, 'dp', 0, 0, tiled=True)  20 us
    pallas_call x1, Pallas kernels, feed_forward(): pl.pallas_call(ffn_kernel, grid=(rows // block,), in_specs=[pl.BlockSpec(...  6.78 us
    ppermute x1, starting transfers between devices, shards(): other = lax.ppermute(partial, 'z_hi', swap)  4.03 us
    ppermute x1, waiting for transfers between devices, shards(): other = lax.ppermute(partial, 'z_hi', swap)  2.34 us
    ppermute x1, waiting for transfers between devices, shards(): got_2 = lax.ppermute(give_2, 'core', swap)  1.98 us
  transfers between devices with their start and end apart: 5, of which 3 were waited for; matrix products, arithmetic and copies ran while one was open for 0% of the time, Pallas kernels for 28%

profile of v4, /device:TPU:0, one launch (start us, length us, event | category | flops | bytes accessed | tf_op | source)
XLA Modules:
  0.0 95.5 jit_solution(515986637793743776)
XLA Ops:
  0.6 0.0 copy-start
  0.6 0.0 copy-start.1
  0.7 6.8 %ffn.1 = f32[16,1024]{1,0:T(8,128)S(1)} custom-call(bf16[1024,1024]{1,0:T(8,128)(2,1)} %bitcast.17, f32[1,1024]{1,0:T(1,128)} %bitcast.18, bf16[1024,1024]{1,0:T(8,128)(2,1)} %win_ref.1, bf16[1024,1024]{1,0:T(8,128)(2,1)} %wout_hbm.1), custom_call_target="tpu_custom_call" | custom-call | flops 2147483648 | bytes 6291456 | tf_op jit(solution)/shard_map/ffn/pallas_call | solution.py:98
  7.4 0.1 collective-permute-start
  7.5 1.2 %collective-permute-done = f32[16,1024]{1,0:T(8,128)S(1)} collective-permute-done((f32[16,1024]{1,0:T(8,128)S(1)}, f32[16,1024]{1,0:T(8,128)S(1)}, u32[]{:S(2)}, u32[]{:S(2)}) %collective-permute-start) | collective-permute-done | bytes 65568 | tf_op jit(solution)/shard_map/ppermute | solution.py:507
  8.8 4.0 %collective-permute-start.1 = (f32[16,1024]{1,0:T(8,128)S(1)}, f32[16,1024]{1,0:T(8,128)S(1)}, u32[]{:S(2)}, u32[]{:S(2)}) collective-permute-start(f32[16,1024]{1,0:T(8,128)S(1)} %add.11.mine_ref), channel_id=1, source_target_pairs={{0,64},{64,0},{1,65},{65,1},{2,66},{66,2},{3,67},{67,3},{4,68},{68... | collective-permute-start | bytes 196616 | tf_op jit(solution)/shard_map/ppermute | solution.py:508
  12.8 0.1 pad_add_fusion.where_ref
  12.9 2.3 %collective-permute-done.1.other_ref = f32[16,1024]{1,0:T(8,128)S(1)} collective-permute-done((f32[16,1024]{1,0:T(8,128)S(1)}, f32[16,1024]{1,0:T(8,128)S(1)}, u32[]{:S(2)}, u32[]{:S(2)}) %collective-permute-start.1) | collective-permute-done | bytes 65568 | tf_op jit(solution)/shard_map/ppermute | solution.py:508
  15.2 0.0 copy-done
  15.2 0.0 copy-done.1
  15.2 0.9 unit_rows.1
  16.1 20.0 %all_to_all.22 = bf16[32,8,1152]{2,1,0:T(8,128)(2,1)S(1)} all-to-all(bf16[32,8,1152]{2,1,0:T(8,128)(2,1)S(1)} %bitcast.15), channel_id=1, replica_groups=mesh['z_hi'=2,'core'=2,'dp'=32] {'dp'}, dimensions={0} | all-to-all | bytes 1179648 | tf_op jit(solution)/shard_map/all_to_all | solution.py:510
  36.1 0.0 collective-permute-start.2
  36.2 14.3 %class_pass.2 = (f32[256,640]{1,0:T(8,128)S(1)}, bf16[256,512]{1,0:T(8,128)(2,1)S(1)}, bf16[256,1152]{1,0:T(8,128)(2,1)S(1)}, f32[1,8192]{1,0:T(1,128)S(1)}) custom-call(s32[3]{0:T(128)S(1)} %pad_add_fusion.where_ref, bf16[256,1152]{1,0:T(8,128)(2,1)S(1)} %bitcast.14, bf16[8192,1024]{1,0:T(8,128)(2,1)} %centres_ref.3), custom_call_target="tpu_custom_call" | custom-call | flops 8589934592 | bytes 16777216 | tf_op jit(solution)/shard_map/class_pass/pallas_call | solution.py:374
  50.5 0.5 collective-permute-start.4
  51.0 0.0 collective-permute-done.2.all_ref
  51.1 12.8 %class_pass.3 = (f32[256,640]{1,0:T(8,128)S(1)}, bf16[256,512]{1,0:T(8,128)(2,1)S(1)}, bf16[256,1152]{1,0:T(8,128)(2,1)S(1)}) custom-call(s32[3]{0:T(128)S(1)} %pad_add_fusion.where_ref, bf16[256,1152]{1,0:T(8,128)(2,1)S(1)} %collective-permute-done.2.all_ref, bf16[8192,1024]{1,0:T(8,128)(2,1)} %centres_ref.3, f32[1,8192]{1,0:T(1,128)S(1)} %get-tuple-element.17.refs_0_), custom_call_target="tpu_custom_call" | custom-call | flops 8589934592 | bytes 16777216 | tf_op jit(solution)/shard_map/class_pass/pallas_call | solution.py:374
  63.9 0.1 collective-permute-start.3
  64.0 0.0 collective-permute-done.4.refs_5_
  64.0 2.0 %collective-permute-done.3.refs_2_ = bf16[256,1152]{1,0:T(8,128)(2,1)S(1)} collective-permute-done((bf16[256,1152]{1,0:T(8,128)(2,1)S(1)}, bf16[256,1152]{1,0:T(8,128)(2,1)S(1)}, u32[]{:S(2)}, u32[]{:S(2)}) %collective-permute-start.3) | collective-permute-done | bytes 589856 | tf_op jit(solution)/shard_map/ppermute | solution.py:515
  66.0 1.4 %pair_sum.1 = bf16[512,1152]{1,0:T(8,128)(2,1)S(1)} custom-call(s32[3]{0:T(128)S(1)} %pad_add_fusion.where_ref, f32[256,640]{1,0:T(8,128)S(1)} %get-tuple-element.15.refs_0_, bf16[256,512]{1,0:T(8,128)(2,1)S(1)} %get-tuple-element.16.refs_1_, bf16[256,1152]{1,0:T(8,128)(2,1)S(1)} %collective-permute-done.3.refs_2_, ...), custom_call_target="tpu_custom_call" | custom-call | tf_op jit(solution)/shard_map/pair_sum/pallas_call | solution.py:434
  67.4 26.6 %all_to_all.23 = bf16[64,8,1152]{2,1,0:T(8,128)(2,1)S(1)} all-to-all(bf16[64,8,1152]{2,1,0:T(8,128)(2,1)S(1)} %bitcast.12), channel_id=1, replica_groups=mesh['z_hi'=2,'core'=2,'dp'=32] {'z_hi','dp'}, dimensions={0} | all-to-all | bytes 2359296 | tf_op jit(solution)/shard_map/all_to_all | solution.py:517
  94.0 1.6 %home.1 = (f32[1,16]{1,0:T(1,128)}, f32[16,256]{1,0:T(8,128)}) custom-call(s32[3]{0:T(128)S(1)} %pad_add_fusion.where_ref, bf16[512,1152]{1,0:T(8,128)(2,1)S(1)} %bitcast.11, f32[16,1024]{1,0:T(8,128)S(1)} %get-tuple-element.22.unit_ref, f32[16,128]{1,0:T(8,128)S(1)} %get-tuple-element.23.len_ref), custom_call_target="tpu_custom_call" | custom-call | tf_op jit(solution)/shard_map/home/pallas_call | solution.py:475
  (1 shorter events, 0.0 us)
Async XLA Ops:
  0.6 14.6 %copy-start = (f32[1024]{0:T(1024)S(1)}, f32[1024]{0:T(1024)}, u32[]{:S(2)}) copy-start(f32[1024]{0:T(1024)} %param.11) | copy-start | bytes 12292
  0.6 14.6 %copy-start.1 = (s32[16]{0:T(128)S(1)}, s32[16]{0:T(128)}, u32[]{:S(2)}) copy-start(s32[16]{0:T(128)} %labels_ref.1) | copy-start | bytes 196
  7.4 1.3 %collective-permute-start = (f32[16,1024]{1,0:T(8,128)S(1)}, f32[16,1024]{1,0:T(8,128)S(1)}, u32[]{:S(2)}, u32[]{:S(2)}) collective-permute-start(f32[16,1024]{1,0:T(8,128)S(1)} %ffn.1), channel_id=1, source_target_pairs={{0,32},{32,0},{1,33},{33,1},{2,34},{34,2},{3,35},{35,3},{4,36},{36... | collective-permute-start | bytes 196616 | tf_op jit(solution)/shard_map/ppermute | solution.py:507
  8.8 6.4 %collective-permute-start.1 = (f32[16,1024]{1,0:T(8,128)S(1)}, f32[16,1024]{1,0:T(8,128)S(1)}, u32[]{:S(2)}, u32[]{:S(2)}) collective-permute-start(f32[16,1024]{1,0:T(8,128)S(1)} %add.11.mine_ref), channel_id=1, source_target_pairs={{0,64},{64,0},{1,65},{65,1},{2,66},{66,2},{3,67},{67,3},{4,68},{68... | collective-permute-start | bytes 196616 | tf_op jit(solution)/shard_map/ppermute | solution.py:508
  36.1 14.9 %collective-permute-start.2 = (bf16[256,1152]{1,0:T(8,128)(2,1)S(1)}, bf16[256,1152]{1,0:T(8,128)(2,1)S(1)}, u32[]{:S(2)}, u32[]{:S(2)}) collective-permute-start(bf16[256,1152]{1,0:T(8,128)(2,1)S(1)} %bitcast.13), channel_id=1, source_target_pairs={{0,32},{32,0},{1,33},{33,1},{2,34},{34,2},{3,35},{35,3},{4,36},{36... | collective-permute-start | bytes 1769480 | tf_op jit(solution)/shard_map/ppermute | solution.py:511
  50.5 13.5 %collective-permute-start.4 = (bf16[256,1152]{1,0:T(8,128)(2,1)S(1)}, bf16[256,1152]{1,0:T(8,128)(2,1)S(1)}, u32[]{:S(2)}, u32[]{:S(2)}) collective-permute-start(bf16[256,1152]{1,0:T(8,128)(2,1)S(1)} %get-tuple-element.21), channel_id=1, source_target_pairs={{0,32},{32,0},{1,33},{33,1},{2,34},{34,2},{3,35},{35,3},{4,36},{36... | collective-permute-start | bytes 1769480 | tf_op jit(solution)/shard_map/ppermute | solution.py:513
  63.9 2.1 %collective-permute-start.3 = (bf16[256,1152]{1,0:T(8,128)(2,1)S(1)}, bf16[256,1152]{1,0:T(8,128)(2,1)S(1)}, u32[]{:S(2)}, u32[]{:S(2)}) collective-permute-start(bf16[256,1152]{1,0:T(8,128)(2,1)S(1)} %get-tuple-element.18), channel_id=1, source_target_pairs={{0,32},{32,0},{1,33},{33,1},{2,34},{34,2},{3,35},{35,3},{4,36},{36... | collective-permute-start | bytes 1769480 | tf_op jit(solution)/shard_map/ppermute | solution.py:515

commit v5 on v4

--- a/solution.py
+++ b/solution.py
@@ -405,26 +405,26 @@
     out_ref = refs[-1]
     rows, half = refs[1].shape
     width, part = 2 * half, half // 2
-    sums, targets, extras = [], [], []
-    for keep_ref, keep_row_ref, got_ref in (refs[0:3], refs[3:6]):
-        sums.append((keep_ref[:, :half] + got_ref[:, :half].astype(f32)).astype(bf16))
-        targets.append(keep_row_ref[...] + got_ref[:, half:width])
+    core = where_ref[1]
+    extras = []
+    for h, (keep_ref, keep_row_ref, got_ref) in ((1 - core, refs[0:3]), (core, refs[3:6])):
+        summed = (keep_ref[:, :half] + got_ref[:, :half].astype(f32)).astype(bf16)
+        target = keep_row_ref[...] + got_ref[:, half:width]
         extras.append(keep_ref[:, half:] + got_ref[:, width:].astype(f32))
-    swapped = where_ref[1] == 0
+        sum_at = pl.ds(pl.multiple_of(h * part, part), part)
+        target_at = pl.ds(pl.multiple_of(half + h * part, part), part)
+        for group in range(2):
+            at = slice(group * rows, (group + 1) * rows)
+            cols = slice(group * part, (group + 1) * part)
+            out_ref[at, sum_at] = summed[:, cols]
+            out_ref[at, target_at] = target[:, cols]
+    swapped = core == 0
     extra = pack_extra(
         [
             unpack_extra(jnp.where(swapped, extras[1 - h], extras[h]), 1)[0]
             for h in range(2)
         ]
     ).astype(bf16)
-    for h in range(2):
-        summed = jnp.where(swapped, sums[1 - h], sums[h])
-        target = jnp.where(swapped, targets[1 - h], targets[h])
-        for group in range(2):
-            at = slice(group * rows, (group + 1) * rows)
-            cols = slice(group * part, (group + 1) * part)
-            out_ref[at, h * part : (h + 1) * part] = summed[:, cols]
-            out_ref[at, half + h * part : half + (h + 1) * part] = target[:, cols]
     for group in range(2):
         out_ref[group * rows : (group + 1) * rows, width:] = extra
 

time: 95.6 us -> 95.8 us (level)
  no operation moved by 1% of the time
where the time goes in v5:
time: 95.8 us; the launch traced here: 95.5 us
  blocking collectives  46.6 us (49%)
  Pallas kernels  37.5 us (39%)
  waiting for transfers between devices  5.55 us (6%)
  starting transfers between devices  5.03 us (5%)
    pallas_call x2, Pallas kernels, class_pass(): pl.pallas_call(functools.partial(class_kernel, second), in_specs=[pl.Bloc...  26.9 us
    all_to_all x1, blocking collectives, shards(): arrived = lax.all_to_all(paired, ('z_hi', 'dp'), 0, 0, tiled=True)  26.6 us
    all_to_all x1, blocking collectives, shards(): gathered = lax.all_to_all(send, 'dp', 0, 0, tiled=True)  20 us
    pallas_call x1, Pallas kernels, feed_forward(): pl.pallas_call(ffn_kernel, grid=(rows // block,), in_specs=[pl.BlockSpec(...  6.78 us
    ppermute x1, starting transfers between devices, shards(): other = lax.ppermute(partial, 'z_hi', swap)  4.03 us
    ppermute x1, waiting for transfers between devices, shards(): other = lax.ppermute(partial, 'z_hi', swap)  2.34 us
    ppermute x1, waiting for transfers between devices, shards(): got_2 = lax.ppermute(give_2, 'core', swap)  1.98 us
  transfers between devices with their start and end apart: 5, of which 3 were waited for; matrix products, arithmetic and copies ran while one was open for 0% of the time, Pallas kernels for 28%

profile of v5, /device:TPU:0, one launch (start us, length us, event | category | flops | bytes accessed | tf_op | source)
XLA Modules:
  0.0 95.5 jit_solution(1114887533782505304)
XLA Ops:
  0.6 0.0 copy-start
  0.6 0.0 copy-start.1
  0.7 6.8 %ffn.1 = f32[16,1024]{1,0:T(8,128)S(1)} custom-call(bf16[1024,1024]{1,0:T(8,128)(2,1)} %bitcast.17, f32[1,1024]{1,0:T(1,128)} %bitcast.18, bf16[1024,1024]{1,0:T(8,128)(2,1)} %win_ref.1, bf16[1024,1024]{1,0:T(8,128)(2,1)} %wout_hbm.1), custom_call_target="tpu_custom_call" | custom-call | flops 2147483648 | bytes 6291456 | tf_op jit(solution)/shard_map/ffn/pallas_call | solution.py:98
  7.4 0.1 collective-permute-start
  7.5 1.2 %collective-permute-done = f32[16,1024]{1,0:T(8,128)S(1)} collective-permute-done((f32[16,1024]{1,0:T(8,128)S(1)}, f32[16,1024]{1,0:T(8,128)S(1)}, u32[]{:S(2)}, u32[]{:S(2)}) %collective-permute-start) | collective-permute-done | bytes 65568 | tf_op jit(solution)/shard_map/ppermute | solution.py:507
  8.8 4.0 %collective-permute-start.1 = (f32[16,1024]{1,0:T(8,128)S(1)}, f32[16,1024]{1,0:T(8,128)S(1)}, u32[]{:S(2)}, u32[]{:S(2)}) collective-permute-start(f32[16,1024]{1,0:T(8,128)S(1)} %add.11.mine_ref), channel_id=1, source_target_pairs={{0,64},{64,0},{1,65},{65,1},{2,66},{66,2},{3,67},{67,3},{4,68},{68... | collective-permute-start | bytes 196616 | tf_op jit(solution)/shard_map/ppermute | solution.py:508
  12.8 0.1 pad_add_fusion.where_ref
  12.9 2.3 %collective-permute-done.1.other_ref = f32[16,1024]{1,0:T(8,128)S(1)} collective-permute-done((f32[16,1024]{1,0:T(8,128)S(1)}, f32[16,1024]{1,0:T(8,128)S(1)}, u32[]{:S(2)}, u32[]{:S(2)}) %collective-permute-start.1) | collective-permute-done | bytes 65568 | tf_op jit(solution)/shard_map/ppermute | solution.py:508
  15.2 0.0 copy-done
  15.2 0.0 copy-done.1
  15.2 0.9 unit_rows.1
  16.1 20.0 %all_to_all.22 = bf16[32,8,1152]{2,1,0:T(8,128)(2,1)S(1)} all-to-all(bf16[32,8,1152]{2,1,0:T(8,128)(2,1)S(1)} %bitcast.15), channel_id=1, replica_groups=mesh['z_hi'=2,'core'=2,'dp'=32] {'dp'}, dimensions={0} | all-to-all | bytes 1179648 | tf_op jit(solution)/shard_map/all_to_all | solution.py:510
  36.1 0.0 collective-permute-start.2
  36.2 14.3 %class_pass.2 = (f32[256,640]{1,0:T(8,128)S(1)}, bf16[256,512]{1,0:T(8,128)(2,1)S(1)}, bf16[256,1152]{1,0:T(8,128)(2,1)S(1)}, f32[1,8192]{1,0:T(1,128)S(1)}) custom-call(s32[3]{0:T(128)S(1)} %pad_add_fusion.where_ref, bf16[256,1152]{1,0:T(8,128)(2,1)S(1)} %bitcast.14, bf16[8192,1024]{1,0:T(8,128)(2,1)} %centres_ref.3), custom_call_target="tpu_custom_call" | custom-call | flops 8589934592 | bytes 16777216 | tf_op jit(solution)/shard_map/class_pass/pallas_call | solution.py:374
  50.5 0.8 collective-permute-start.4
  51.3 0.0 collective-permute-done.2.all_ref
  51.3 12.6 %class_pass.3 = (f32[256,640]{1,0:T(8,128)S(1)}, bf16[256,512]{1,0:T(8,128)(2,1)S(1)}, bf16[256,1152]{1,0:T(8,128)(2,1)S(1)}) custom-call(s32[3]{0:T(128)S(1)} %pad_add_fusion.where_ref, bf16[256,1152]{1,0:T(8,128)(2,1)S(1)} %collective-permute-done.2.all_ref, bf16[8192,1024]{1,0:T(8,128)(2,1)} %centres_ref.3, f32[1,8192]{1,0:T(1,128)S(1)} %get-tuple-element.17.refs_0_), custom_call_target="tpu_custom_call" | custom-call | flops 8589934592 | bytes 16777216 | tf_op jit(solution)/shard_map/class_pass/pallas_call | solution.py:374
  63.9 0.1 collective-permute-start.3
  64.0 0.0 collective-permute-done.4.refs_5_
  64.0 2.0 %collective-permute-done.3.refs_2_ = bf16[256,1152]{1,0:T(8,128)(2,1)S(1)} collective-permute-done((bf16[256,1152]{1,0:T(8,128)(2,1)S(1)}, bf16[256,1152]{1,0:T(8,128)(2,1)S(1)}, u32[]{:S(2)}, u32[]{:S(2)}) %collective-permute-start.3) | collective-permute-done | bytes 589856 | tf_op jit(solution)/shard_map/ppermute | solution.py:515
  66.0 1.3 %pair_sum.1 = bf16[512,1152]{1,0:T(8,128)(2,1)S(1)} custom-call(s32[3]{0:T(128)S(1)} %pad_add_fusion.where_ref, f32[256,640]{1,0:T(8,128)S(1)} %get-tuple-element.15.refs_0_, bf16[256,512]{1,0:T(8,128)(2,1)S(1)} %get-tuple-element.16.refs_1_, bf16[256,1152]{1,0:T(8,128)(2,1)S(1)} %collective-permute-done.3.refs_2_, ...), custom_call_target="tpu_custom_call" | custom-call | tf_op jit(solution)/shard_map/pair_sum/pallas_call | solution.py:434
  67.3 26.6 %all_to_all.23 = bf16[64,8,1152]{2,1,0:T(8,128)(2,1)S(1)} all-to-all(bf16[64,8,1152]{2,1,0:T(8,128)(2,1)S(1)} %bitcast.12), channel_id=1, replica_groups=mesh['z_hi'=2,'core'=2,'dp'=32] {'z_hi','dp'}, dimensions={0} | all-to-all | bytes 2359296 | tf_op jit(solution)/shard_map/all_to_all | solution.py:517
  93.9 1.6 %home.1 = (f32[1,16]{1,0:T(1,128)}, f32[16,256]{1,0:T(8,128)}) custom-call(s32[3]{0:T(128)S(1)} %pad_add_fusion.where_ref, bf16[512,1152]{1,0:T(8,128)(2,1)S(1)} %bitcast.11, f32[16,1024]{1,0:T(8,128)S(1)} %get-tuple-element.22.unit_ref, f32[16,128]{1,0:T(8,128)S(1)} %get-tuple-element.23.len_ref), custom_call_target="tpu_custom_call" | custom-call | tf_op jit(solution)/shard_map/home/pallas_call | solution.py:475
  (1 shorter events, 0.0 us)
Async XLA Ops:
  0.6 14.6 %copy-start = (f32[1024]{0:T(1024)S(1)}, f32[1024]{0:T(1024)}, u32[]{:S(2)}) copy-start(f32[1024]{0:T(1024)} %param.11) | copy-start | bytes 12292
  0.6 14.6 %copy-start.1 = (s32[16]{0:T(128)S(1)}, s32[16]{0:T(128)}, u32[]{:S(2)}) copy-start(s32[16]{0:T(128)} %labels_ref.1) | copy-start | bytes 196
  7.4 1.3 %collective-permute-start = (f32[16,1024]{1,0:T(8,128)S(1)}, f32[16,1024]{1,0:T(8,128)S(1)}, u32[]{:S(2)}, u32[]{:S(2)}) collective-permute-start(f32[16,1024]{1,0:T(8,128)S(1)} %ffn.1), channel_id=1, source_target_pairs={{0,32},{32,0},{1,33},{33,1},{2,34},{34,2},{3,35},{35,3},{4,36},{36... | collective-permute-start | bytes 196616 | tf_op jit(solution)/shard_map/ppermute | solution.py:507
  8.8 6.4 %collective-permute-start.1 = (f32[16,1024]{1,0:T(8,128)S(1)}, f32[16,1024]{1,0:T(8,128)S(1)}, u32[]{:S(2)}, u32[]{:S(2)}) collective-permute-start(f32[16,1024]{1,0:T(8,128)S(1)} %add.11.mine_ref), channel_id=1, source_target_pairs={{0,64},{64,0},{1,65},{65,1},{2,66},{66,2},{3,67},{67,3},{4,68},{68... | collective-permute-start | bytes 196616 | tf_op jit(solution)/shard_map/ppermute | solution.py:508
  36.1 15.2 %collective-permute-start.2 = (bf16[256,1152]{1,0:T(8,128)(2,1)S(1)}, bf16[256,1152]{1,0:T(8,128)(2,1)S(1)}, u32[]{:S(2)}, u32[]{:S(2)}) collective-permute-start(bf16[256,1152]{1,0:T(8,128)(2,1)S(1)} %bitcast.13), channel_id=1, source_target_pairs={{0,32},{32,0},{1,33},{33,1},{2,34},{34,2},{3,35},{35,3},{4,36},{36... | collective-permute-start | bytes 1769480 | tf_op jit(solution)/shard_map/ppermute | solution.py:511
  50.5 13.5 %collective-permute-start.4 = (bf16[256,1152]{1,0:T(8,128)(2,1)S(1)}, bf16[256,1152]{1,0:T(8,128)(2,1)S(1)}, u32[]{:S(2)}, u32[]{:S(2)}) collective-permute-start(bf16[256,1152]{1,0:T(8,128)(2,1)S(1)} %get-tuple-element.21), channel_id=1, source_target_pairs={{0,32},{32,0},{1,33},{33,1},{2,34},{34,2},{3,35},{35,3},{4,36},{36... | collective-permute-start | bytes 1769480 | tf_op jit(solution)/shard_map/ppermute | solution.py:513
  63.9 2.1 %collective-permute-start.3 = (bf16[256,1152]{1,0:T(8,128)(2,1)S(1)}, bf16[256,1152]{1,0:T(8,128)(2,1)S(1)}, u32[]{:S(2)}, u32[]{:S(2)}) collective-permute-start(bf16[256,1152]{1,0:T(8,128)(2,1)S(1)} %get-tuple-element.18), channel_id=1, source_target_pairs={{0,32},{32,0},{1,33},{33,1},{2,34},{34,2},{3,35},{35,3},{4,36},{36... | collective-permute-start | bytes 1769480 | tf_op jit(solution)/shard_map/ppermute | solution.py:515

commit v6 on v4

--- a/solution.py
+++ b/solution.py
@@ -346,18 +346,19 @@
     return out
 
 
-def unpack_extra(extra, halves_held):
-    halves = []
-    for h in range(halves_held):
-        values = []
-        for k in range(3 * h, 3 * h + 3):
-            values.append(
-                extra[:, 3 * k : 3 * k + 1]
-                + extra[:, 3 * k + 1 : 3 * k + 2]
-                + extra[:, 3 * k + 2 : 3 * k + 3]
+def unpack_extra(extra):
+    lane = lax.broadcasted_iota(jnp.int32, extra.shape, 1)
+    return [
+        [
+            jnp.sum(
+                jnp.where(jnp.logical_and(lane // 64 == h, lane % 16 // 3 == k), extra, 0.0),
+                axis=1,
+                keepdims=True,
             )
-        halves.append(values)
-    return halves
+            for k in range(3)
+        ]
+        for h in range(2)
+    ]
 
 
 def class_pass(where, gathered, centres, inverse=None):
@@ -411,12 +412,11 @@
         targets.append(keep_row_ref[...] + got_ref[:, half:width])
         extras.append(keep_ref[:, half:] + got_ref[:, width:].astype(f32))
     swapped = where_ref[1] == 0
-    extra = pack_extra(
-        [
-            unpack_extra(jnp.where(swapped, extras[1 - h], extras[h]), 1)[0]
-            for h in range(2)
-        ]
-    ).astype(bf16)
+    spread = []
+    for h in range(2):
+        hi, mid, low = split3(jnp.where(swapped, extras[1 - h], extras[h]))
+        spread.append(hi + pltpu.roll(mid, 16, 1) + pltpu.roll(low, 32, 1))
+    extra = (spread[0] + pltpu.roll(spread[1], 64, 1)).astype(bf16)
     for h in range(2):
         summed = jnp.where(swapped, sums[1 - h], sums[h])
         target = jnp.where(swapped, targets[1 - h], targets[h])
@@ -452,7 +452,7 @@
     row = lax.broadcasted_iota(jnp.int32, (half, images), 0)
     lane = lax.broadcasted_iota(jnp.int32, (half, images), 1)
     loss_row = jnp.zeros((1, images), f32)
-    for h, (rest, inner, cos) in enumerate(unpack_extra(summed[:, 4 * part :], 2)):
+    for h, (rest, inner, cos) in enumerate(unpack_extra(summed[:, 4 * part :])):
         at = slice(h * half, (h + 1) * half)
         gradient = summed[:, h * part : (h + 1) * part]
         target = summed[:, (2 + h) * part : (3 + h) * part]

time: 95.6 us -> 95.2 us (level)
  Pallas kernels: 37.8 us -> 36.7 us
where the time goes in v6:
time: 95.2 us; the launch traced here: 95 us
  blocking collectives  47 us (49%)
  Pallas kernels  36.7 us (39%)
  starting transfers between devices  5.29 us (6%)
  waiting for transfers between devices  5.2 us (5%)
    all_to_all x1, blocking collectives, shards(): arrived = lax.all_to_all(paired, ('z_hi', 'dp'), 0, 0, tiled=True)  26.9 us
    pallas_call x2, Pallas kernels, class_pass(): pl.pallas_call(functools.partial(class_kernel, second), in_specs=[pl.Bloc...  26.6 us
    all_to_all x1, blocking collectives, shards(): gathered = lax.all_to_all(send, 'dp', 0, 0, tiled=True)  20 us
    pallas_call x1, Pallas kernels, feed_forward(): pl.pallas_call(ffn_kernel, grid=(rows // block,), in_specs=[pl.BlockSpec(...  6.78 us
    ppermute x1, starting transfers between devices, shards(): other = lax.ppermute(partial, 'z_hi', swap)  4.03 us
    ppermute x1, waiting for transfers between devices, shards(): other = lax.ppermute(partial, 'z_hi', swap)  2.34 us
  transfers between devices with their start and end apart: 5, of which 3 were waited for; matrix products, arithmetic and copies ran while one was open for 0% of the time, Pallas kernels for 28%

profile of v6, /device:TPU:0, one launch (start us, length us, event | category | flops | bytes accessed | tf_op | source)
XLA Modules:
  0.0 95.0 jit_solution(14952229996315810567)
XLA Ops:
  0.6 0.0 copy-start
  0.6 0.0 copy-start.1
  0.7 6.8 %ffn.1 = f32[16,1024]{1,0:T(8,128)S(1)} custom-call(bf16[1024,1024]{1,0:T(8,128)(2,1)} %bitcast.17, f32[1,1024]{1,0:T(1,128)} %bitcast.18, bf16[1024,1024]{1,0:T(8,128)(2,1)} %win_ref.1, bf16[1024,1024]{1,0:T(8,128)(2,1)} %wout_hbm.1), custom_call_target="tpu_custom_call" | custom-call | flops 2147483648 | bytes 6291456 | tf_op jit(solution)/shard_map/ffn/pallas_call | solution.py:98
  7.4 0.1 collective-permute-start
  7.5 1.2 %collective-permute-done = f32[16,1024]{1,0:T(8,128)S(1)} collective-permute-done((f32[16,1024]{1,0:T(8,128)S(1)}, f32[16,1024]{1,0:T(8,128)S(1)}, u32[]{:S(2)}, u32[]{:S(2)}) %collective-permute-start) | collective-permute-done | bytes 65568 | tf_op jit(solution)/shard_map/ppermute | solution.py:507
  8.8 4.0 %collective-permute-start.1 = (f32[16,1024]{1,0:T(8,128)S(1)}, f32[16,1024]{1,0:T(8,128)S(1)}, u32[]{:S(2)}, u32[]{:S(2)}) collective-permute-start(f32[16,1024]{1,0:T(8,128)S(1)} %add.11.mine_ref), channel_id=1, source_target_pairs={{0,64},{64,0},{1,65},{65,1},{2,66},{66,2},{3,67},{67,3},{4,68},{68... | collective-permute-start | bytes 196616 | tf_op jit(solution)/shard_map/ppermute | solution.py:508
  12.8 0.1 pad_add_fusion.where_ref
  12.9 2.3 %collective-permute-done.1.other_ref = f32[16,1024]{1,0:T(8,128)S(1)} collective-permute-done((f32[16,1024]{1,0:T(8,128)S(1)}, f32[16,1024]{1,0:T(8,128)S(1)}, u32[]{:S(2)}, u32[]{:S(2)}) %collective-permute-start.1) | collective-permute-done | bytes 65568 | tf_op jit(solution)/shard_map/ppermute | solution.py:508
  15.2 0.0 copy-done
  15.2 0.0 copy-done.1
  15.2 0.9 unit_rows.1
  16.1 20.0 %all_to_all.22 = bf16[32,8,1152]{2,1,0:T(8,128)(2,1)S(1)} all-to-all(bf16[32,8,1152]{2,1,0:T(8,128)(2,1)S(1)} %bitcast.15), channel_id=1, replica_groups=mesh['z_hi'=2,'core'=2,'dp'=32] {'dp'}, dimensions={0} | all-to-all | bytes 1179648 | tf_op jit(solution)/shard_map/all_to_all | solution.py:510
  36.1 0.0 collective-permute-start.2
  36.2 14.4 %class_pass.2 = (f32[256,640]{1,0:T(8,128)S(1)}, bf16[256,512]{1,0:T(8,128)(2,1)S(1)}, bf16[256,1152]{1,0:T(8,128)(2,1)S(1)}, f32[1,8192]{1,0:T(1,128)S(1)}) custom-call(s32[3]{0:T(128)S(1)} %pad_add_fusion.where_ref, bf16[256,1152]{1,0:T(8,128)(2,1)S(1)} %bitcast.14, bf16[8192,1024]{1,0:T(8,128)(2,1)} %centres_ref.3), custom_call_target="tpu_custom_call" | custom-call | flops 8589934592 | bytes 16777216 | tf_op jit(solution)/shard_map/class_pass/pallas_call | solution.py:375
  50.5 0.5 collective-permute-start.4
  51.0 0.0 collective-permute-done.2.all_ref
  51.1 12.3 %class_pass.3 = (f32[256,640]{1,0:T(8,128)S(1)}, bf16[256,512]{1,0:T(8,128)(2,1)S(1)}, bf16[256,1152]{1,0:T(8,128)(2,1)S(1)}) custom-call(s32[3]{0:T(128)S(1)} %pad_add_fusion.where_ref, bf16[256,1152]{1,0:T(8,128)(2,1)S(1)} %collective-permute-done.2.all_ref, bf16[8192,1024]{1,0:T(8,128)(2,1)} %centres_ref.3, f32[1,8192]{1,0:T(1,128)S(1)} %get-tuple-element.17.refs_0_), custom_call_target="tpu_custom_call" | custom-call | flops 8589934592 | bytes 16777216 | tf_op jit(solution)/shard_map/class_pass/pallas_call | solution.py:375
  63.4 0.6 collective-permute-start.3
  64.0 0.0 collective-permute-done.4.refs_5_
  64.0 1.6 %collective-permute-done.3.refs_2_ = bf16[256,1152]{1,0:T(8,128)(2,1)S(1)} collective-permute-done((bf16[256,1152]{1,0:T(8,128)(2,1)S(1)}, bf16[256,1152]{1,0:T(8,128)(2,1)S(1)}, u32[]{:S(2)}, u32[]{:S(2)}) %collective-permute-start.3) | collective-permute-done | bytes 589856 | tf_op jit(solution)/shard_map/ppermute | solution.py:515
  65.6 1.1 %pair_sum.1 = bf16[512,1152]{1,0:T(8,128)(2,1)S(1)} custom-call(s32[3]{0:T(128)S(1)} %pad_add_fusion.where_ref, f32[256,640]{1,0:T(8,128)S(1)} %get-tuple-element.15.refs_0_, bf16[256,512]{1,0:T(8,128)(2,1)S(1)} %get-tuple-element.16.refs_1_, bf16[256,1152]{1,0:T(8,128)(2,1)S(1)} %collective-permute-done.3.refs_2_, ...), custom_call_target="tpu_custom_call" | custom-call | tf_op jit(solution)/shard_map/pair_sum/pallas_call | solution.py:434
  66.7 26.9 %all_to_all.23 = bf16[64,8,1152]{2,1,0:T(8,128)(2,1)S(1)} all-to-all(bf16[64,8,1152]{2,1,0:T(8,128)(2,1)S(1)} %bitcast.12), channel_id=1, replica_groups=mesh['z_hi'=2,'core'=2,'dp'=32] {'z_hi','dp'}, dimensions={0} | all-to-all | bytes 2359296 | tf_op jit(solution)/shard_map/all_to_all | solution.py:517
  93.7 1.3 %home.1 = (f32[1,16]{1,0:T(1,128)}, f32[16,256]{1,0:T(8,128)}) custom-call(s32[3]{0:T(128)S(1)} %pad_add_fusion.where_ref, bf16[512,1152]{1,0:T(8,128)(2,1)S(1)} %bitcast.11, f32[16,1024]{1,0:T(8,128)S(1)} %get-tuple-element.22.unit_ref, f32[16,128]{1,0:T(8,128)S(1)} %get-tuple-element.23.len_ref), custom_call_target="tpu_custom_call" | custom-call | tf_op jit(solution)/shard_map/home/pallas_call | solution.py:475
  (1 shorter events, 0.0 us)
Async XLA Ops:
  0.6 14.6 %copy-start = (f32[1024]{0:T(1024)S(1)}, f32[1024]{0:T(1024)}, u32[]{:S(2)}) copy-start(f32[1024]{0:T(1024)} %param.11) | copy-start | bytes 12292
  0.6 14.6 %copy-start.1 = (s32[16]{0:T(128)S(1)}, s32[16]{0:T(128)}, u32[]{:S(2)}) copy-start(s32[16]{0:T(128)} %labels_ref.1) | copy-start | bytes 196
  7.4 1.3 %collective-permute-start = (f32[16,1024]{1,0:T(8,128)S(1)}, f32[16,1024]{1,0:T(8,128)S(1)}, u32[]{:S(2)}, u32[]{:S(2)}) collective-permute-start(f32[16,1024]{1,0:T(8,128)S(1)} %ffn.1), channel_id=1, source_target_pairs={{0,32},{32,0},{1,33},{33,1},{2,34},{34,2},{3,35},{35,3},{4,36},{36... | collective-permute-start | bytes 196616 | tf_op jit(solution)/shard_map/ppermute | solution.py:507
  8.8 6.4 %collective-permute-start.1 = (f32[16,1024]{1,0:T(8,128)S(1)}, f32[16,1024]{1,0:T(8,128)S(1)}, u32[]{:S(2)}, u32[]{:S(2)}) collective-permute-start(f32[16,1024]{1,0:T(8,128)S(1)} %add.11.mine_ref), channel_id=1, source_target_pairs={{0,64},{64,0},{1,65},{65,1},{2,66},{66,2},{3,67},{67,3},{4,68},{68... | collective-permute-start | bytes 196616 | tf_op jit(solution)/shard_map/ppermute | solution.py:508
  36.1 14.9 %collective-permute-start.2 = (bf16[256,1152]{1,0:T(8,128)(2,1)S(1)}, bf16[256,1152]{1,0:T(8,128)(2,1)S(1)}, u32[]{:S(2)}, u32[]{:S(2)}) collective-permute-start(bf16[256,1152]{1,0:T(8,128)(2,1)S(1)} %bitcast.13), channel_id=1, source_target_pairs={{0,32},{32,0},{1,33},{33,1},{2,34},{34,2},{3,35},{35,3},{4,36},{36... | collective-permute-start | bytes 1769480 | tf_op jit(solution)/shard_map/ppermute | solution.py:511
  50.5 13.5 %collective-permute-start.4 = (bf16[256,1152]{1,0:T(8,128)(2,1)S(1)}, bf16[256,1152]{1,0:T(8,128)(2,1)S(1)}, u32[]{:S(2)}, u32[]{:S(2)}) collective-permute-start(bf16[256,1152]{1,0:T(8,128)(2,1)S(1)} %get-tuple-element.21), channel_id=1, source_target_pairs={{0,32},{32,0},{1,33},{33,1},{2,34},{34,2},{3,35},{35,3},{4,36},{36... | collective-permute-start | bytes 1769480 | tf_op jit(solution)/shard_map/ppermute | solution.py:513
  63.4 2.3 %collective-permute-start.3 = (bf16[256,1152]{1,0:T(8,128)(2,1)S(1)}, bf16[256,1152]{1,0:T(8,128)(2,1)S(1)}, u32[]{:S(2)}, u32[]{:S(2)}) collective-permute-start(bf16[256,1152]{1,0:T(8,128)(2,1)S(1)} %get-tuple-element.18), channel_id=1, source_target_pairs={{0,32},{32,0},{1,33},{33,1},{2,34},{34,2},{3,35},{35,3},{4,36},{36... | collective-permute-start | bytes 1769480 | tf_op jit(solution)/shard_map/ppermute | solution.py:515
